TPU v7x, 256 devices: a whole 4x4x8 slice. The times are simulated.
256 devices in a mesh: dp: 32 (over x, z_lo, y), tensor: 8 (over z_hi, core).
Axes of the slice: x: 4, y: 4, z: 8 (z_hi: 4, z_lo: 2; z = z_hi * 2 + z_lo), core: 2. Of those that a mesh axis runs over, the one named last changes fastest.
Arguments:
- hidden_input_rows: bfloat16 [4096, 8192], P('dp'), may hold values from -6 to 6
- output_gradient: bfloat16 [4096, 8192], P('dp', 'tensor'), may hold values from -6 to 6
- gate_activation: bfloat16 [4096, 28672], P(None, ('dp', 'tensor')), may hold values from -0.25 to 2.5
- down_projection_codes: int32 [28672, 8192], P('dp', 'tensor'), may hold values from 0 to 15
- block_scale_codes: int32 [448, 8192], P('dp', 'tensor'), may hold values from 0 to 255
- outer_level_scales: float32 [448, 128], P('dp', 'tensor'), may hold values from 0.03 to 0.08
- adapter_down_factor: bfloat16 [16, 8192], replicated, may hold values from -0.0625 to 0.0625
- adapter_up_factor: bfloat16 [16, 28672], P(None, 'dp'), may hold values from -0.03125 to 0.03125
- query_down_gradient: bfloat16 [128, 16, 8192], P('dp', None, 'tensor'), may hold values from -0.0014648438 to 0.0014648438
- query_up_gradient: bfloat16 [128, 16, 28672], P(None, None, ('dp', 'tensor')), may hold values from -0.0007324219 to 0.0007324219
Outputs:
- scores: float32 [32, 128], P('dp', 'tensor')
Inputs may be any that keep to these rules, and one draw needn't show every extreme that they name: `down_projection_codes`: index into the sixteen NF4 levels. `block_scale_codes`: 8-bit scale code.
All inputs are finite; a program needn't handle non-finite values.
Results may differ from a plain program's by a relative error of at most 0.014.
Values may be sent and summed in bfloat16 or wider, within the bound.
A program may use at most 128 MiB of HBM per device.

v0:
```python
import jax
import jax.numpy as jnp
from jax import lax
from jax.sharding import PartitionSpec as P

BLOCK = 64
GROUP = 64


levels = (
    -1.0,
    -0.6961928009986877,
    -0.5250730514526367,
    -0.39491748809814453,
    -0.28444138169288635,
    -0.18477343022823334,
    -0.09105003625154495,
    0.0,
    0.07958029955625534,
    0.16093020141124725,
    0.24611230194568634,
    0.33791524171829224,
    0.44070982933044434,
    0.5626170039176941,
    0.7229568362236023,
    1.0,
)


def dequantize(codes, block_codes, second_scales):
    values = jnp.zeros(codes.shape, jnp.float32)
    for level_index in range(16):
        values = jnp.where(codes == level_index, jnp.float32(levels[level_index]), values)
    column_scale = jnp.repeat(second_scales, GROUP, axis=1)
    scaling = (block_codes + 1).astype(jnp.float32) / 256.0 * column_scale
    row_count = codes.shape[0]
    col_count = codes.shape[1]
    values = values.reshape(row_count // BLOCK, BLOCK, col_count) * scaling[:, None, :]
    return values.reshape(row_count, col_count).astype(jnp.bfloat16)


def split_pair(values):
    upper = values.astype(jnp.bfloat16)
    lower = (values - upper.astype(jnp.float32)).astype(jnp.bfloat16)
    return (upper, lower)


def contract_final_axis(left, right):
    return lax.dot_general(
        left, right, (((1,), (1,)), ((), ())), preferred_element_type=jnp.float32
    )


def contract_split(values, right):
    upper, lower = split_pair(values)
    return contract_final_axis(upper, right) + contract_final_axis(lower, right)


def per_example(upward, projection, seq_len):
    example_count = upward.shape[0] // seq_len
    upper, lower = split_pair(upward)
    shaped_proj = projection.reshape(example_count, seq_len, projection.shape[1])
    shaped_upper = upper.reshape(example_count, seq_len, upward.shape[1])
    shaped_lower = lower.reshape(example_count, seq_len, upward.shape[1])
    first = jnp.einsum(
        "esr,esf->erf", shaped_proj, shaped_upper, preferred_element_type=jnp.float32
    )
    second = jnp.einsum(
        "esr,esf->erf", shaped_proj, shaped_lower, preferred_element_type=jnp.float32
    )
    return first + second


def shards(
    hidden_input_rows,
    output_gradient,
    gate_activation,
    down_projection_codes,
    block_scale_codes,
    outer_level_scales,
    adapter_down_factor,
    adapter_up_factor,
    query_down_gradient,
    query_up_gradient,
):
    seq_len = hidden_input_rows.shape[0]
    feature_width = output_gradient.shape[1]
    tensor_count = lax.axis_size("tensor")
    tensor_shard_rank = lax.axis_index("tensor")
    data_rank = lax.axis_index("dp")
    weights = dequantize(down_projection_codes, block_scale_codes, outer_level_scales)
    low_rank_product = contract_final_axis(hidden_input_rows, adapter_down_factor).astype(
        jnp.bfloat16
    )
    cot_all, proj_all = (
        lax.all_gather(output_gradient, "dp", axis=0, tiled=True),
        lax.all_gather(low_rank_product, "dp", axis=0, tiled=True),
    )
    partial_value = contract_final_axis(cot_all, weights)
    example_count = cot_all.shape[0] // seq_len
    hidden_unit_width = partial_value.shape[1] // tensor_count
    hidden_grad = lax.psum_scatter(partial_value, "tensor", scatter_dimension=1, tiled=True)
    upward = hidden_grad * gate_activation.astype(jnp.float32)
    factor_window = lax.dynamic_slice_in_dim(
        adapter_up_factor, tensor_shard_rank * hidden_unit_width, hidden_unit_width, 1
    )
    grad_full = per_example(upward, proj_all, seq_len)
    factor_part = contract_split(upward, factor_window)
    grad_b = grad_full.astype(jnp.bfloat16)
    query_count = query_up_gradient.shape[0]
    score_b = contract_final_axis(
        grad_b.reshape(example_count, -1), query_up_gradient.reshape(query_count, -1)
    )
    factor_all = lax.psum(factor_part, ("dp", "tensor"))
    factor_rows = lax.dynamic_slice_in_dim(factor_all, data_rank * seq_len, seq_len, 0)
    input_slice = lax.dynamic_slice_in_dim(
        hidden_input_rows, tensor_shard_rank * feature_width, feature_width, 1
    )
    factor_upper, factor_lower = split_pair(factor_rows)
    transposed = (((0,), (0,)), ((), ()))
    grad_a = (
        lax.dot_general(factor_upper, input_slice, transposed, preferred_element_type=jnp.float32)
        + lax.dot_general(factor_lower, input_slice, transposed, preferred_element_type=jnp.float32)
    ).astype(jnp.bfloat16)
    flat_grad = grad_a.reshape(1, -1)
    piece = lax.all_gather(query_down_gradient, "dp", axis=0, tiled=True)
    part = contract_final_axis(flat_grad, piece.reshape(piece.shape[0], -1))
    row_mask = (jnp.arange(example_count) == data_rank)[:, None]
    score_a = jnp.where(row_mask, part, jnp.float32(0.0))
    combined = (score_a + score_b).reshape(1, -1)
    owned = lax.psum_scatter(combined, ("dp", "tensor"), scatter_dimension=1, tiled=True)
    return owned


def solution(mesh):
    in_specs = (
        P("dp", None),
        P("dp", "tensor"),
        P(None, ("dp", "tensor")),
        P("dp", "tensor"),
        P("dp", "tensor"),
        P("dp", "tensor"),
        P(),
        P(None, "dp"),
        P("dp", None, "tensor"),
        P(None, None, ("dp", "tensor")),
    )
    out_specs = P("dp", "tensor")
    return jax.shard_map(shards, mesh=mesh, in_specs=in_specs, out_specs=out_specs, check_vma=False)
```

profile of v0, /device:TPU:1, one launch (start us, length us, event | category | flops | bytes accessed | tf_op | source)
XLA Modules:
  0.0 2052.6 jit_solution(3661330714019908245)
XLA Ops:
  6.5 0.0 copy-start
  6.5 0.0 all-gather.3.cloned.1.call-start
  6.5 0.7 all-gather.3.cloned.1.call-update
  7.3 0.0 reduce-scatter.5.cloned.1.call-start
  7.3 0.8 broadcast_in_dim.92
  8.1 0.1 reshape.31
  8.2 0.9 multiply_multiply_fusion
  9.0 6.5 fusion.2
  15.6 148.1 %all-gather.3.cloned.1.call-done = bf16[4096,1024]{1,0:T(8,128)(2,1)} async-done(((bf16[128,1024]{1,0:T(8,128)(2,1)}), bf16[4096,1024]{1,0:T(8,128)(2,1)}) %all-gather.3.cloned.1.call-update) | async-done | bytes 8388624 | tf_op jit(solution)/shard_map/all_gather | solution.py:96
  163.7 14.7 convolution_bitcast_fusion
  178.4 0.0 copy-start.3
  178.4 0.0 reduce-scatter.5.cloned.1.call-update
  178.4 0.0 copy-start.5
  178.4 0.0 all-reduce.2.cloned.1.call-start
  178.5 173.6 %reduce-scatter.5.cloned.1.call-done = f32[4096,112]{0,1:T(8,128)} async-done(((f32[4096,896]{0,1:T(8,128)}), f32[4096,112]{0,1:T(8,128)}) %reduce-scatter.5.cloned.1.call-update) | async-done | bytes 1835024 | tf_op jit(solution)/shard_map/reduce_scatter | solution.py:102
  352.1 0.0 copy-done.3
  352.1 0.0 copy-start.1
  352.1 2.0 fusion.18
  354.0 0.1 copy-done.1
  354.1 1.7 convolution_add_fusion
  355.9 0.0 all-reduce.2.cloned.1.call-update
  355.9 0.0 all-gather.5.cloned.1.call-start
  355.9 0.5 all-gather.5.cloned.1.call-update
  356.5 0.0 reduce-scatter.7.cloned.1.call-start
  356.5 0.0 copy-done
  356.5 0.0 copy-done.5
  356.6 0.0 copy-start.2
  356.6 0.6 convolution_convert_fusion
  357.2 64.2 %all_gather.11 = bf16[4096,16]{0,1:T(8,128)(2,1)S(1)} all-gather(bf16[128,16]{0,1:T(8,128)(2,1)S(1)} %convolution_convert_fusion), channel_id=1, replica_groups=mesh['dp'=32,'tensor'=8] {'dp'}, dimensions={0}, use_global_device_ids=true | all-gather | bytes 135168 | tf_op jit(solution)/shard_map/all_gather | solution.py:97
  421.4 0.0 copy-done.2
  421.4 0.5 fusion.17
  421.9 0.0 copy-start.4
  421.9 0.6 fusion.10
  422.5 0.6 fusion.13
  423.1 185.2 %all-reduce.2.cloned.1.call-done = f32[4096,16]{0,1:T(8,128)} async-done(((f32[4096,16]{0,1:T(8,128)}), f32[4096,16]{0,1:T(8,128)}) %all-reduce.2.cloned.1.call-update) | async-done | bytes 262160 | tf_op jit(solution)/shard_map/psum | solution.py:114
  608.2 0.8 fusion.21
  609.1 0.9 fusion.5
  609.9 140.4 %all-gather.5.cloned.1.call-done = bf16[128,16,1024]{2,1,0:T(8,128)(2,1)} async-done(((bf16[4,16,1024]{2,1,0:T(8,128)(2,1)}), bf16[128,16,1024]{2,1,0:T(8,128)(2,1)}) %all-gather.5.cloned.1.call-update) | async-done | bytes 4194320 | tf_op jit(solution)/shard_map/all_gather | solution.py:126
  750.4 6.7 fusion.7
  757.1 0.0 copy-done.4
  757.1 0.3 fusion.6
  757.4 2.0 copy.18
  759.4 0.0 reduce-scatter.7.cloned.1.call-update
  759.4 1285.4 %reduce-scatter.7.cloned.1.call-done = f32[16,1]{1,0:T(8,128)} async-done(((f32[4096,1]{1,0:T(8,128)}), f32[16,1]{1,0:T(8,128)}) %reduce-scatter.7.cloned.1.call-update) | async-done | bytes 80
  2044.8 1.3 copy.19
  (1 shorter events, 0.0 us)
Async XLA Ops:
  6.5 350.0 %copy-start = (bf16[128,8192]{1,0:T(8,128)(2,1)S(1)}, bf16[128,8192]{1,0:T(8,128)(2,1)}, u32[]{:S(2)}) copy-start(bf16[128,8192]{1,0:T(8,128)(2,1)} %param.10) | copy-start | bytes 6291460
  6.5 157.2 %all-gather.3.cloned.1.call-start = ((), (), s32[]{:S(2)}) async-start(), calls=%async_computation.2 | async-start | bytes 8650752 | tf_op jit(solution)/shard_map/all_gather | solution.py:96
  7.3 344.8 %reduce-scatter.5.cloned.1.call-start = ((), (), s32[]{:S(2)}) async-start(), calls=%async_computation.3 | async-start | bytes 16515072 | tf_op jit(solution)/shard_map/reduce_scatter | solution.py:102
  178.4 173.7 %copy-start.3 = (bf16[4096,112]{0,1:T(8,128)(2,1)S(1)}, bf16[4096,112]{0,1:T(8,128)(2,1)}, u32[]{:S(2)}) copy-start(bf16[4096,112]{0,1:T(8,128)(2,1)} %param.12) | copy-start | bytes 2752516
  178.4 178.1 %copy-start.5 = (bf16[16,8192]{1,0:T(8,128)(2,1)S(1)}, bf16[16,8192]{1,0:T(8,128)(2,1)}, u32[]{:S(2)}) copy-start(bf16[16,8192]{1,0:T(8,128)(2,1)} %param.16) | copy-start | bytes 786436
  178.4 429.8 %all-reduce.2.cloned.1.call-start = ((), (), s32[]{:S(2)}) async-start(), calls=%async_computation.4 | async-start | bytes 524288 | tf_op jit(solution)/shard_map/psum | solution.py:114
  352.1 2.1 copy-start.1
  355.9 394.5 %all-gather.5.cloned.1.call-start = ((), (), s32[]{:S(2)}) async-start(), calls=%async_computation.5 | async-start | bytes 4325376 | tf_op jit(solution)/shard_map/all_gather | solution.py:126
  356.5 1688.4 %reduce-scatter.7.cloned.1.call-start = ((), (), s32[]{:S(2)}) async-start(), calls=%async_computation.6 | async-start | bytes 2105344
  356.6 64.9 %copy-start.2 = (f32[4096,112]{0,1:T(8,128)S(1)}, f32[4096,112]{0,1:T(8,128)}, u32[]{:S(2)}) copy-start(f32[4096,112]{0,1:T(8,128)} %reduce-scatter.5.cloned.1.call-done) | copy-start | bytes 5505028
  421.9 335.2 %copy-start.4 = (bf16[128,16,112]{0,2,1:T(8,128)(2,1)S(1)}, bf16[128,16,112]{0,2,1:T(8,128)(2,1)}, u32[]{:S(2)}) copy-start(bf16[128,16,112]{0,2,1:T(8,128)(2,1)} %param.19) | copy-start | bytes 1376260
Sparse Core Ops, SparseCore 0:
  9.1 154.5 all-gather.2
  178.6 173.4 reduce-scatter.4
  357.5 250.6 all-reduce.1
  609.9 140.4 all-gather.4
  759.6 1285.2 reduce-scatter.6
where the time goes:
time: 2060 us; the launch traced here: 2050 us
  waiting for transfers between devices  1930 us (94%)
  blocking collectives  64.2 us (3%)
  matrix products  28.9 us (1%)
    unnamed x6, waiting for transfers between devices  1290 us
    psum x1, waiting for transfers between devices, shards(): factor_all = lax.psum(factor_part, ('dp', 'tensor'))  185 us
    reduce_scatter x1, waiting for transfers between devices, shards(): lax.psum_scatter(partial_value, 'tensor', scatter_dimension=1, tiled=True)  174 us
    all_gather x1, waiting for transfers between devices, shards(): lax.all_gather(output_gradient, 'dp', axis=0, tiled=True)  148 us
    all_gather x1, waiting for transfers between devices, shards(): piece = lax.all_gather(query_down_gradient, 'dp', axis=0, tiled=True)  140 us
    all_gather x1, blocking collectives, shards(): lax.all_gather(low_rank_product, 'dp', axis=0, tiled=True)  64.2 us
  transfers between devices with their start and end apart: 5, of which 5 were waited for; matrix products, arithmetic and copies ran while one was open for 1% of the time, Pallas kernels for 0%

commit v1 on v0

v1 whole, which is shorter than its diff:
```python
import jax
import jax.numpy as jnp
from jax import lax
from jax.experimental import pallas as pl
from jax.experimental.pallas import tpu as pltpu
from jax.sharding import PartitionSpec as P

MESH = pl.DeviceIdType.MESH
F32 = jnp.float32
BF16 = jnp.bfloat16
NT = (((1,), (1,)), ((), ()))
NN = (((1,), (0,)), ((), ()))
ANY = pl.BlockSpec(memory_space=pl.ANY)

PIECES = 16
SLOTS = 8
STAGES = 4

LEVELS = (
    -1.0,
    -0.6961928009986877,
    -0.5250730514526367,
    -0.39491748809814453,
    -0.28444138169288635,
    -0.18477343022823334,
    -0.09105003625154495,
    0.0,
    0.07958029955625534,
    0.16093020141124725,
    0.24611230194568634,
    0.33791524171829224,
    0.44070982933044434,
    0.5626170039176941,
    0.7229568362236023,
    1.0,
)


def lookup(codes):
    values = [jnp.full(codes.shape, level, F32) for level in LEVELS]
    for bit in range(4):
        odd = (codes & (1 << bit)) != 0
        values = [jnp.where(odd, values[i + 1], values[i]) for i in range(0, len(values), 2)]
    return values[0]


def offset(k):
    return k + k // 2 - 2 * (k // 3)


def piece_uv(n):
    late = jnp.maximum(n - 4, 0)
    first = n < 4
    return jnp.where(first, n, late // 3), jnp.where(first, 0, 1 + late % 3)


def kernel(
    x_hbm, og_hbm, gate_hbm, codes_hbm, bsc_hbm, osc_hbm, ad_hbm, au_hbm, qd_hbm, qu_hbm,
    out_ref,
    buf, qbuf, codes, bsc, osc, scale, w, xs, ad, au, auj, gate, qu, qf, qt,
    prod, own, csend, crecv, rsend, rrecv, proj, gb, fac, t1, t2s, t2, mt, acc, t3s, t3,
    lsem, og_ss, og_rs, qd_ss, qd_rs, c_ss, c_rs, r_ss, r_rs, p_ss, p_rs, t1_ss, t1_rs, t2_ss, t2_rs, t3_ss, t3_rs,
):
    dp = lax.axis_index("dp")
    tn = lax.axis_index("tensor")
    y, l, x = dp % 4, (dp // 4) % 2, dp // 8
    zh, c = tn // 2, tn % 2

    width = og_hbm.shape[1]
    here = x * 4 + y
    loads = [
        (og_hbm.at[pl.ds(0, 64)], buf.at[0, here, l]),
        (og_hbm.at[pl.ds(64, 64)], buf.at[1, here, l]),
        (codes_hbm, codes),
        (bsc_hbm, bsc),
        (osc_hbm, osc),
        (x_hbm, xs),
        (ad_hbm, ad),
        (au_hbm, au),
        (gate_hbm, gate),
        (qd_hbm.at[pl.ds(0, 32)], qbuf.at[0, here, l]),
        (qd_hbm.at[pl.ds(32, 32)], qbuf.at[1, here, l]),
        (qu_hbm, qu),
    ]
    loads = [pltpu.make_async_copy(a, b, lsem.at[i]) for i, (a, b) in enumerate(loads)]
    for load in loads:
        load.start()

    barrier = pltpu.get_barrier_semaphore()

    def greet_dp(o, _):
        pl.semaphore_signal(barrier, 1, device_id={"dp": (dp + o) % 32}, device_id_type=MESH)
        return 0

    def greet_tn(o, _):
        pl.semaphore_signal(barrier, 1, device_id={"tensor": (tn + o) % 8}, device_id_type=MESH)
        return 0

    lax.fori_loop(1, 32, greet_dp, 0)
    lax.fori_loop(1, 8, greet_tn, 0)
    pl.semaphore_wait(barrier, 38)

    def pair_at(k, u, v):
        a, b = offset(u), offset(v)
        if k == 0:
            return ((x + a) % 4) * 4 + (y + b) % 4
        return ((x + b) % 4) * 4 + (y + a) % 4

    def near(k, first, step):
        along_x = first == (k == 0)
        if along_x:
            return {"dp": (((x + step) % 4) * 2 + l) * 4 + y}
        return {"dp": (x * 2 + l) * 4 + (y + step) % 4}

    def piece_copy(data, ss, rs, k, u, v, half, ur, vr, target):
        ref = data.at[k, pair_at(k, u, v), half]
        return pltpu.make_async_remote_copy(
            src_ref=ref, dst_ref=ref, send_sem=ss.at[k, ur, vr, half], recv_sem=rs.at[k, ur, vr, half],
            device_id=target, device_id_type=MESH,
        )

    partner = {"dp": (x * 2 + 1 - l) * 4 + y}

    def gather_start(data, ss, rs):
        for k in range(2):
            piece_copy(data, ss, rs, k, 0, 0, l, 0, 0, partner).start()
            piece_copy(data, ss, rs, k, 0, 0, l, 2, 0, near(k, True, 1)).start()
            piece_copy(data, ss, rs, k, 0, 0, l, 1, 0, near(k, True, 3)).start()

    def gather_second(data, ss, rs, u):
        for k in range(2):
            for half in range(2):
                piece_copy(data, ss, rs, k, u, 0, half, u, 2, near(k, False, 1)).start()
                piece_copy(data, ss, rs, k, u, 0, half, u, 1, near(k, False, 3)).start()

    def gather_step(data, ss, rs, n):
        u, v = piece_uv(n)

        @pl.when(n == 0)
        def _():
            for k in range(2):
                piece_copy(data, ss, rs, k, 0, 0, 1 - l, 0, 0, partner).wait_recv()
                piece_copy(data, ss, rs, k, 0, 0, 1 - l, 2, 0, near(k, True, 1)).start()
                piece_copy(data, ss, rs, k, 0, 0, 1 - l, 1, 0, near(k, True, 3)).start()

        @pl.when(n > 0)
        def _():
            for k in range(2):
                for half in range(2):
                    piece_copy(data, ss, rs, k, u, v, half, u, v, partner).wait_recv()

        @pl.when(n == 1)
        def _():
            for k in range(2):
                piece_copy(data, ss, rs, k, 1, 0, 1, 3, 0, near(k, True, 3)).start()

        @pl.when(n == 2)
        def _():
            for k in range(2):
                piece_copy(data, ss, rs, k, 2, 0, 0, 3, 0, near(k, True, 1)).start()

        @pl.when(v == 1)
        def _():
            for k in range(2):
                piece_copy(data, ss, rs, k, u, 1, 1, u, 3, near(k, False, 3)).start()

        @pl.when(v == 2)
        def _():
            for k in range(2):
                piece_copy(data, ss, rs, k, u, 2, 0, u, 3, near(k, False, 1)).start()

        nxt = jnp.where(n == 1, 0, jnp.where(n == 3, 1, jnp.where(n == 4, 2, 3)))

        @pl.when((n == 1) | (n == 3) | (n == 4) | (n == 7))
        def _():
            gather_second(data, ss, rs, nxt)

    def gather_drain(data, ss, rs):
        def body(i, _):
            u, v = i // 4, i % 4
            for k in range(2):
                for half in range(2):
                    piece_copy(data, ss, rs, k, 0, 0, half, u, v, partner).wait_send()
            return 0

        for k in range(2):
            piece_copy(data, ss, rs, k, 0, 0, l, 0, 0, partner).wait_send()
        lax.fori_loop(1, 16, body, 0)

    og = (buf, og_ss, og_rs)
    qd = (qbuf, qd_ss, qd_rs)

    loads[0].wait()
    loads[1].wait()
    gather_start(*og)

    loads[5].wait()
    loads[6].wait()
    proj[dp] = lax.dot_general(ad[...], xs[...], NT, preferred_element_type=F32).astype(BF16)

    def proj_copy(o, to):
        return pltpu.make_async_remote_copy(
            src_ref=proj.at[dp], dst_ref=proj.at[dp], send_sem=p_ss.at[o], recv_sem=p_rs.at[o],
            device_id={"dp": (dp + o) % 32}, device_id_type=MESH,
        )

    def proj_send(o, _):
        proj_copy(o, None).start()
        return 0

    lax.fori_loop(1, 32, proj_send, 0)

    loads[3].wait()
    loads[4].wait()
    lane14 = lax.broadcasted_iota(jnp.int32, (14, 128), 1)
    for col in range(width // 128):
        pick = jnp.where(
            lane14 < 64,
            jnp.broadcast_to(osc[:, 2 * col : 2 * col + 1], (14, 128)),
            jnp.broadcast_to(osc[:, 2 * col + 1 : 2 * col + 2], (14, 128)),
        )
        at = pl.ds(col * 128, 128)
        scale[:, at] = (bsc[:, at] + 1).astype(F32) / 256.0 * pick
    loads[2].wait()

    def dequant(b, _):
        rows = pl.ds(pl.multiple_of(b * 64, 64), 64)
        w[rows, :] = (lookup(codes[rows, :]) * scale[pl.ds(b, 1), :]).astype(BF16)
        return 0

    lax.fori_loop(0, 14, dequant, 0)

    loads[7].wait()
    mine = jnp.zeros((16, 112), F32)
    for j in range(8):
        mine = jnp.where(tn == j, au[:, j * 112 : (j + 1) * 112].astype(F32), mine)
    auj[...] = mine.astype(BF16)
    gb[...] = jnp.zeros_like(gb)
    fac[...] = jnp.zeros_like(fac)
    loads[8].wait()

    def core_copy(p):
        return pltpu.make_async_remote_copy(
            src_ref=csend.at[p], dst_ref=crecv.at[p], send_sem=c_ss.at[p], recv_sem=c_rs.at[p],
            device_id={"tensor": zh * 2 + 1 - c}, device_id_type=MESH,
        )

    def ring_copy(p, d, i):
        step = 1 if d == 0 else 3
        return pltpu.make_async_remote_copy(
            src_ref=rsend.at[p, d, i], dst_ref=rrecv.at[p, d, i], send_sem=r_ss.at[p, d, i],
            recv_sem=r_rs.at[p, d, i],
            device_id={"tensor": ((zh + step) % 4) * 2 + c}, device_id_type=MESH,
        )

    def ring_target(d, i):
        return (zh + (3 - i if d == 0 else i + 1)) % 4

    def multiply(p):
        u, v = piece_uv(p)
        rows = jnp.concatenate(
            [buf[0, pair_at(0, u, v)].reshape(128, width), buf[1, pair_at(1, u, v)].reshape(128, width)], axis=0
        )
        prod[...] = lax.dot_general(w[...], rows, NT, preferred_element_type=F32).reshape(8, 112, 256)
        slot = p % SLOTS
        for k in range(4):
            csend[p, k] = prod[2 * k + 1 - c].astype(BF16)
            own[slot, k] = prod[2 * k + c]
        core_copy(p).start()

    def core_add(p):
        core_copy(p).wait_recv()
        slot = p % SLOTS
        for k in range(4):
            own[slot, k] += crecv[p, k].astype(F32)
        for d in range(2):
            rsend[p, d, 0] = own[slot, ring_target(d, 0), :, d * 128 : (d + 1) * 128].astype(BF16)
            ring_copy(p, d, 0).start()

    def ring_add(p, i):
        slot = p % SLOTS
        for d in range(2):
            ring_copy(p, d, i - 1).wait_recv()
            part = own[slot, ring_target(d, i), :, d * 128 : (d + 1) * 128]
            rsend[p, d, i] = (part + rrecv[p, d, i - 1].astype(F32)).astype(BF16)
            ring_copy(p, d, i).start()

    lane16 = lax.broadcasted_iota(jnp.int32, (16, 128), 1)
    low = lane16 < 64
    eye = (
        lax.broadcasted_iota(jnp.int32, (112, 112), 0) == lax.broadcasted_iota(jnp.int32, (112, 112), 1)
    ).astype(F32).astype(BF16)

    def finish(p):
        u, v = piece_uv(p)
        slot = p % SLOTS
        for d in range(2):
            ring_copy(p, d, 2).wait_recv()
            hidden = own[slot, zh, :, d * 128 : (d + 1) * 128] + rrecv[p, d, 2].astype(F32)
            pair = pair_at(d, u, v)
            e0 = (pair // 4) * 8 + pair % 4
            e1 = e0 + 4
            rows = jnp.concatenate(
                [gate[pl.ds(pl.multiple_of(e * 128 + d * 64, 64), 64), :] for e in (e0, e1)], axis=0
            )
            gate_t = lax.dot_general(eye, rows, NT, preferred_element_type=F32)
            up = (hidden * gate_t).astype(BF16)
            ft = lax.dot_general(auj[...], up, NN, preferred_element_type=F32)
            turned = pltpu.roll(ft, 64, 1)
            p0, p1 = proj[e0].astype(F32), proj[e1].astype(F32)
            zero = jnp.zeros_like(p0)
            if d == 0:
                fac[e0, 0:16] += jnp.where(low, ft, 0.0)
                fac[e1, 0:16] += jnp.where(low, turned, 0.0)
                q0 = jnp.where(low, p0, zero)
                q1 = jnp.where(low, zero, pltpu.roll(p1, 64, 1))
            else:
                fac[e0, 0:16] += jnp.where(low, 0.0, turned)
                fac[e1, 0:16] += jnp.where(low, 0.0, ft)
                q0 = jnp.where(low, pltpu.roll(p0, 64, 1), zero)
                q1 = jnp.where(low, zero, p1)
            both = jnp.concatenate([q0, q1], axis=0).astype(BF16)
            grad = lax.dot_general(both, up, NT, preferred_element_type=F32)
            r0 = pl.ds(pl.multiple_of(e0 * 16, 16), 16)
            r1 = pl.ds(pl.multiple_of(e1 * 16, 16), 16)
            gb[r0, :] += grad[0:16]
            gb[r1, :] += grad[16:32]

    def og_due(s):
        return jnp.minimum(1 + (4 * s + 2) // 3, 16)

    def qd_due(s):
        return jnp.clip((s - 11) * 2, 0, 16)

    gather_step(*og, 0)

    def iteration(s, _):
        @pl.when((s >= 2) & (s - 2 < PIECES))
        def _():
            ring_add(s - 2, 1)

        @pl.when((s >= 3) & (s - 3 < PIECES))
        def _():
            ring_add(s - 3, 2)

        @pl.when((s >= 1) & (s - 1 < PIECES))
        def _():
            core_add(s - 1)

        @pl.when(s < PIECES)
        def _():
            multiply(s)

        def og_step(n, _):
            gather_step(*og, n)
            return 0

        lax.fori_loop(og_due(s), og_due(s + 1), og_step, 0)

        @pl.when(s == 11)
        def _():
            loads[9].wait()
            loads[10].wait()
            gather_start(*qd)

        def qd_step(n, _):
            gather_step(*qd, n)
            return 0

        lax.fori_loop(qd_due(s), qd_due(s + 1), qd_step, 0)

        @pl.when(s == STAGES)
        def _():
            def proj_wait(o, _):
                proj_copy(o, None).wait_recv()
                return 0

            lax.fori_loop(1, 32, proj_wait, 0)

        @pl.when(s >= STAGES)
        def _():
            finish(s - STAGES)

        return 0

    loads[11].wait()
    qf[...] = qu[...].astype(F32).reshape(2048, 112)
    for r in range(16):
        qt[r] = qf[pl.ds(r, 128, stride=16), :].astype(BF16)

    lax.fori_loop(0, PIECES + STAGES, iteration, 0)

    score_b = jnp.zeros((32, 128), F32)
    for r in range(16):
        part = gb[pl.ds(r, 32, stride=16), :].astype(BF16)
        score_b += lax.dot_general(part, qt[r], NT, preferred_element_type=F32)
    fac[:, 16:24, :] = jnp.broadcast_to(score_b[:, None, :], (32, 8, 128))

    def t1_copy(o):
        return pltpu.make_async_remote_copy(
            src_ref=fac.at[(dp + o) % 32], dst_ref=t1.at[o], send_sem=t1_ss.at[o], recv_sem=t1_rs.at[o],
            device_id={"dp": (dp + o) % 32}, device_id_type=MESH,
        )

    def t1_send(o, _):
        t1_copy(o).start()
        return 0

    lax.fori_loop(1, 32, t1_send, 0)

    xd = xs[:, pl.ds(pl.multiple_of(tn * width, 128), width)]

    def meet(i, _):
        k, a = i // 4, i % 4
        rows = qbuf[k, pl.ds(a * 4, 4)].reshape(256, width)
        part = lax.dot_general(rows, xd, NT, preferred_element_type=F32).reshape(4, 2, 32, 128)
        for b in range(4):
            for half in range(2):
                start = ((a * 2 + half) * 4 + b) * 64 + k * 32
                mt[pl.ds(pl.multiple_of(start, 32), 32), :] = part[b, half]
        return 0

    lax.fori_loop(0, 8, meet, 0)
    gather_drain(*og)
    gather_drain(*qd)

    def drain(p, _):
        core_copy(p).wait_send()
        for d in range(2):
            for i in range(3):
                ring_copy(p, d, i).wait_send()
        return 0

    lax.fori_loop(0, PIECES, drain, 0)

    def proj_drain(o, _):
        proj_copy(o, None).wait_send()
        return 0

    lax.fori_loop(1, 32, proj_drain, 0)

    def t1_take(o, total):
        t1_copy(o).wait_recv()
        return total + t1[o]

    total = lax.fori_loop(1, 32, t1_take, fac[dp])

    def t2_copy(o):
        return pltpu.make_async_remote_copy(
            src_ref=t2s, dst_ref=t2.at[o], send_sem=t2_ss.at[o], recv_sem=t2_rs.at[o],
            device_id={"tensor": (tn + o) % 8}, device_id_type=MESH,
        )

    def t3_copy(o):
        return pltpu.make_async_remote_copy(
            src_ref=t3s, dst_ref=t3.at[o], send_sem=t3_ss.at[o], recv_sem=t3_rs.at[o],
            device_id={"tensor": (tn + o) % 8}, device_id_type=MESH,
        )

    t2s[...] = total[0:16]
    for o in range(1, 8):
        t2_copy(o).start()

    def t1_drain(o, _):
        t1_copy(o).wait_send()
        return 0

    lax.fori_loop(1, 32, t1_drain, 0)
    factors = total[0:16]
    for o in range(1, 8):
        t2_copy(o).wait_recv()
        factors += t2[o]

    def weigh(i, _):
        rows = mt[pl.ds(pl.multiple_of(i * 128, 128), 128), :].reshape(8, 16, 128)
        acc[pl.ds(pl.multiple_of(i * 8, 8), 8), :] = jnp.sum(rows * factors[None], axis=1)
        return 0

    lax.fori_loop(0, 16, weigh, 0)
    score_a = lax.dot_general(
        jnp.ones((8, 128), F32), acc[...], NT, precision=lax.Precision.HIGHEST, preferred_element_type=F32
    )
    t3s[...] = total[16:24] + score_a
    for o in range(1, 8):
        t3_copy(o).start()
    for o in range(1, 8):
        t2_copy(o).wait_send()
    scores = t3s[...]
    for o in range(1, 8):
        t3_copy(o).wait_recv()
        scores += t3[o]
    out = jnp.zeros((1, 16), F32)
    for j in range(8):
        out = jnp.where(tn == j, scores[0:1, j * 16 : (j + 1) * 16], out)
    out_ref[...] = out
    for o in range(1, 8):
        t3_copy(o).wait_send()


def shards(x, og, gate, codes, bsc, osc, ad, au, qd, qu):
    qd = qd.reshape(64, 1024)
    dma = pltpu.SemaphoreType.DMA
    vmem = pltpu.VMEM
    return pl.pallas_call(
        kernel,
        out_shape=jax.ShapeDtypeStruct((1, 16), F32),
        in_specs=[ANY] * 10,
        out_specs=pl.BlockSpec(memory_space=pltpu.VMEM),
        scratch_shapes=[
            vmem((2, 16, 2, 64, 1024), BF16),
            vmem((2, 16, 2, 32, 1024), BF16),
            vmem((896, 1024), jnp.int32),
            vmem((14, 1024), jnp.int32),
            vmem((14, 16), F32),
            vmem((14, 1024), F32),
            vmem((896, 1024), BF16),
            vmem((128, 8192), BF16),
            vmem((16, 8192), BF16),
            vmem((16, 896), BF16),
            vmem((16, 112), BF16),
            vmem((4096, 112), BF16),
            vmem((128, 16, 112), BF16),
            vmem((2048, 112), F32),
            vmem((16, 128, 112), BF16),
            vmem((8, 112, 256), F32),
            vmem((SLOTS, 4, 112, 256), F32),
            vmem((PIECES, 4, 112, 256), BF16),
            vmem((PIECES, 4, 112, 256), BF16),
            vmem((PIECES, 2, 3, 112, 128), BF16),
            vmem((PIECES, 2, 3, 112, 128), BF16),
            vmem((32, 16, 128), BF16),
            vmem((512, 112), F32),
            vmem((32, 24, 128), F32),
            vmem((32, 24, 128), F32),
            vmem((16, 128), F32),
            vmem((8, 16, 128), F32),
            vmem((2048, 128), F32),
            vmem((128, 128), F32),
            vmem((8, 128), F32),
            vmem((8, 8, 128), F32),
            dma((12,)),
            dma((2, 4, 4, 2)),
            dma((2, 4, 4, 2)),
            dma((2, 4, 4, 2)),
            dma((2, 4, 4, 2)),
            dma((PIECES,)),
            dma((PIECES,)),
            dma((PIECES, 2, 3)),
            dma((PIECES, 2, 3)),
            dma((32,)),
            dma((32,)),
            dma((32,)),
            dma((32,)),
            dma((8,)),
            dma((8,)),
            dma((8,)),
            dma((8,)),
        ],
        compiler_params=pltpu.CompilerParams(
            collective_id=0, has_side_effects=True, vmem_limit_bytes=60 * 1024 * 1024
        ),
        name="influence",
    )(x, og, gate, codes, bsc, osc, ad, au, qd, qu)


def solution(mesh):
    in_specs = (
        P("dp", None),
        P("dp", "tensor"),
        P(None, ("dp", "tensor")),
        P("dp", "tensor"),
        P("dp", "tensor"),
        P("dp", "tensor"),
        P(),
        P(None, "dp"),
        P("dp", None, "tensor"),
        P(None, None, ("dp", "tensor")),
    )
    return jax.shard_map(shards, mesh=mesh, in_specs=in_specs, out_specs=P("dp", "tensor"), check_vma=False)
```

time: 2060 us -> 168 us (0.08)
  waiting for transfers between devices: 1930 us -> 0 us
  Pallas kernels: 0 us -> 163 us
  blocking collectives: 64.2 us -> 0 us
  matrix products: 28.9 us -> 0 us
    unnamed x6 -> x0, waiting for transfers between devices: 1290 us -> none
    all_gather x2 -> x0, waiting for transfers between devices: 289 us -> none  [the longest x1 148 us: shards(): lax.all_gather(output_gradient, 'dp', axis=0, tiled=True)]
    psum x1 -> x0, waiting for transfers between devices: 185 us -> none  [shards(): factor_all = lax.psum(factor_part, ('dp', 'tensor'))]
    reduce_scatter x1 -> x0, waiting for transfers between devices: 174 us -> none  [shards(): lax.psum_scatter(partial_value, 'tensor', scatter_dimension=1, tiled=True)]
    pallas_call x0 -> x1, Pallas kernels: none -> 163 us  [shards(): pl.pallas_call(kernel, out_shape=jax.ShapeDtypeStruct((1, 16), F32), in_s...]
    all_gather x1 -> x0, blocking collectives: 64.2 us -> none  [shards(): lax.all_gather(low_rank_product, 'dp', axis=0, tiled=True)]
    dot_general x10 -> x0, matrix products: 28.9 us -> none  [the longest x6 26.1 us: contract_final_axis(): lax.dot_general(left, right, (((1,), (1,)), ((), ())), preferred_element_...]
  transfers between devices with their start and end apart: 5 -> 0, of which waited for: 5 -> 0; matrix products, arithmetic and copies ran while one was open for 1% -> 0% of each run, Pallas kernels for 0% -> 0%
where the time goes in v1:
time: 168 us
  Pallas kernels  163 us (97%)
  local copies, waits for them, and re-layouts  5.64 us (3%)
    pallas_call x1, Pallas kernels, shards(): pl.pallas_call(kernel, out_shape=jax.ShapeDtypeStruct((1, 16), F32), in_s...  163 us
    unnamed x3, local copies, waits for them, and re-layouts  5.64 us

profile of v1, /device:TPU:1, one launch (start us, length us, event | category | flops | bytes accessed | tf_op | source)
XLA Modules:
  0.0 168.2 jit_solution(13745640562589233785)
XLA Ops:
  0.0 2.2 %copy.12.qu_hbm = bf16[128,16,112]{2,1,0:T(8,128)(2,1)} copy(bf16[128,16,112]{0,2,1:T(8,128)(2,1)} %param.19) | data formatting | bytes 917504 | tf_op args[9]
  2.2 2.3 %copy.11.gate_hbm = bf16[4096,112]{1,0:T(8,128)(2,1)} copy(bf16[4096,112]{0,1:T(8,128)(2,1)} %param.12) | data formatting | bytes 1835008 | tf_op args[2]
  4.5 162.6 %influence.1 = f32[1,16]{1,0:T(1,128)} custom-call(bf16[128,8192]{1,0:T(8,128)(2,1)} %x_hbm.1, bf16[128,1024]{1,0:T(8,128)(2,1)} %og_hbm.1, bf16[4096,112]{1,0:T(8,128)(2,1)} %copy.11.gate_hbm, s32[896,1024]{1,0:T(8,128)} %codes_hbm.1, s32[14,1024]{1,0:T(8,128)} %bsc_hbm.1, f32[14,16]{1,0:T(8,128)} %osc_hbm.1, bf16[16,8192]{1,0:T(8,128)(2,1)} %ad_hbm.1, ...), custom_call_target="tpu_custom_call" | custom-call | tf_op jit(solution)/shard_map/influence/pallas_call | solution.py:504
  167.1 1.1 copy.14

commit v2 on v1

--- a/solution.py
+++ b/solution.py
@@ -14,7 +14,8 @@
 
 PIECES = 16
 SLOTS = 8
-STAGES = 4
+LAG = 2
+STAGES = 1 + 3 * LAG
 
 LEVELS = (
     -1.0,
@@ -48,18 +49,53 @@
     return k + k // 2 - 2 * (k // 3)
 
 
+ORDER = (
+    (0, 0), (1, 0), (2, 0), (0, 1), (0, 2), (3, 0), (0, 3), (1, 1),
+    (1, 2), (2, 1), (2, 2), (1, 3), (3, 1), (3, 2), (2, 3), (3, 3),
+)
+
+
 def piece_uv(n):
-    late = jnp.maximum(n - 4, 0)
-    first = n < 4
-    return jnp.where(first, n, late // 3), jnp.where(first, 0, 1 + late % 3)
+    u = v = 0
+    for i, (a, b) in enumerate(ORDER):
+        u = jnp.where(n == i, a, u)
+        v = jnp.where(n == i, b, v)
+    return u, v
+
+
+OG_BEFORE = {1: [("take", 1, 0)]}
+OG_AFTER = {
+    1: [("take", 2, 0), ("take", 0, 1), ("take", 0, 2), ("second", 1)],
+    2: [("second", 2)],
+    3: [("take", 3, 0)],
+    4: [("second", 3), ("take", 0, 3)],
+    5: [("take", 1, 1), ("take", 1, 2)],
+    7: [("take", 2, 1), ("take", 2, 2)],
+    8: [("take", 1, 3)],
+    9: [("take", 3, 1), ("take", 3, 2)],
+    10: [("take", 2, 3)],
+    12: [("take", 3, 3)],
+}
+QD_AFTER = {
+    8: [("start",)],
+    9: [("take", 0, 0)],
+    11: [("take", 1, 0), ("take", 2, 0), ("take", 0, 1), ("take", 0, 2), ("second", 1)],
+    12: [("second", 2)],
+    13: [("take", 3, 0), ("second", 3), ("take", 0, 3)],
+    14: [("take", 1, 1), ("take", 1, 2)],
+    16: [("take", 2, 1), ("take", 2, 2)],
+    18: [("take", 3, 1), ("take", 3, 2)],
+    19: [("take", 1, 3), ("take", 2, 3)],
+    21: [("take", 3, 3)],
+}
 
 
 def kernel(
     x_hbm, og_hbm, gate_hbm, codes_hbm, bsc_hbm, osc_hbm, ad_hbm, au_hbm, qd_hbm, qu_hbm,
     out_ref,
-    buf, qbuf, codes, bsc, osc, scale, w, xs, ad, au, auj, gate, qu, qf, qt,
-    prod, own, csend, crecv, rsend, rrecv, proj, gb, fac, t1, t2s, t2, mt, acc, t3s, t3,
-    lsem, og_ss, og_rs, qd_ss, qd_rs, c_ss, c_rs, r_ss, r_rs, p_ss, p_rs, t1_ss, t1_rs, t2_ss, t2_rs, t3_ss, t3_rs,
+    buf, qbuf, codes, bsc, osc, scale, w, xs, ad, au, auj, gate, qu,
+    prod, own, csend, crecv, rsend, rrecv, proj, gb, fac, t1, t2s, t2, sbs, t1b, mt, acc, t3s, t3,
+    lsem, og_ss, og_rs, qd_ss, qd_rs, c_ss, c_rs, r_ss, r_rs, p_ss, p_rs, t1_ss, t1_rs, t1b_ss, t1b_rs, t2_ss, t2_rs, t3_ss, t3_rs,
 ):
     dp = lax.axis_index("dp")
     tn = lax.axis_index("tensor")
@@ -113,79 +149,61 @@
         return {"dp": (x * 2 + l) * 4 + (y + step) % 4}
 
     def piece_copy(data, ss, rs, k, u, v, half, ur, vr, target):
-        ref = data.at[k, pair_at(k, u, v), half]
-        return pltpu.make_async_remote_copy(
-            src_ref=ref, dst_ref=ref, send_sem=ss.at[k, ur, vr, half], recv_sem=rs.at[k, ur, vr, half],
+        ref = data.at[k, pair_at(k, u, v)]
+        sem = 0 if half is None else half
+        ref = ref if half is None else ref.at[half]
+        return pltpu.make_async_remote_copy(
+            src_ref=ref, dst_ref=ref, send_sem=ss.at[k, ur, vr, sem], recv_sem=rs.at[k, ur, vr, sem],
             device_id=target, device_id_type=MESH,
         )
 
     partner = {"dp": (x * 2 + 1 - l) * 4 + y}
+
+    def halves(u, v):
+        return (0, 1) if u == 0 or v == 0 or v == 3 else (None,)
+
+    def gather_own(data, ss, rs, k, half):
+        piece_copy(data, ss, rs, k, 0, 0, half, 2, 0, near(k, True, 1)).start()
+        piece_copy(data, ss, rs, k, 0, 0, half, 1, 0, near(k, True, 3)).start()
+        piece_copy(data, ss, rs, k, 0, 0, half, 0, 2, near(k, False, 1)).start()
+        piece_copy(data, ss, rs, k, 0, 0, half, 0, 1, near(k, False, 3)).start()
 
     def gather_start(data, ss, rs):
         for k in range(2):
             piece_copy(data, ss, rs, k, 0, 0, l, 0, 0, partner).start()
-            piece_copy(data, ss, rs, k, 0, 0, l, 2, 0, near(k, True, 1)).start()
-            piece_copy(data, ss, rs, k, 0, 0, l, 1, 0, near(k, True, 3)).start()
+        for k in range(2):
+            gather_own(data, ss, rs, k, l)
 
     def gather_second(data, ss, rs, u):
         for k in range(2):
-            for half in range(2):
-                piece_copy(data, ss, rs, k, u, 0, half, u, 2, near(k, False, 1)).start()
-                piece_copy(data, ss, rs, k, u, 0, half, u, 1, near(k, False, 3)).start()
-
-    def gather_step(data, ss, rs, n):
-        u, v = piece_uv(n)
-
-        @pl.when(n == 0)
-        def _():
-            for k in range(2):
+            piece_copy(data, ss, rs, k, u, 0, None, u, 2, near(k, False, 1)).start()
+            piece_copy(data, ss, rs, k, u, 0, None, u, 1, near(k, False, 3)).start()
+
+    def gather_take(data, ss, rs, u, v):
+        for k in range(2):
+            if (u, v) == (0, 0):
                 piece_copy(data, ss, rs, k, 0, 0, 1 - l, 0, 0, partner).wait_recv()
-                piece_copy(data, ss, rs, k, 0, 0, 1 - l, 2, 0, near(k, True, 1)).start()
-                piece_copy(data, ss, rs, k, 0, 0, 1 - l, 1, 0, near(k, True, 3)).start()
-
-        @pl.when(n > 0)
-        def _():
-            for k in range(2):
-                for half in range(2):
-                    piece_copy(data, ss, rs, k, u, v, half, u, v, partner).wait_recv()
-
-        @pl.when(n == 1)
-        def _():
-            for k in range(2):
-                piece_copy(data, ss, rs, k, 1, 0, 1, 3, 0, near(k, True, 3)).start()
-
-        @pl.when(n == 2)
-        def _():
-            for k in range(2):
-                piece_copy(data, ss, rs, k, 2, 0, 0, 3, 0, near(k, True, 1)).start()
-
-        @pl.when(v == 1)
-        def _():
-            for k in range(2):
-                piece_copy(data, ss, rs, k, u, 1, 1, u, 3, near(k, False, 3)).start()
-
-        @pl.when(v == 2)
-        def _():
-            for k in range(2):
-                piece_copy(data, ss, rs, k, u, 2, 0, u, 3, near(k, False, 1)).start()
-
-        nxt = jnp.where(n == 1, 0, jnp.where(n == 3, 1, jnp.where(n == 4, 2, 3)))
-
-        @pl.when((n == 1) | (n == 3) | (n == 4) | (n == 7))
-        def _():
-            gather_second(data, ss, rs, nxt)
+                gather_own(data, ss, rs, k, 1 - l)
+                continue
+            for half in halves(u, v):
+                piece_copy(data, ss, rs, k, u, v, half, u, v, partner).wait_recv()
+            if v == 0 and u < 3:
+                half = 2 - u
+                piece_copy(data, ss, rs, k, u, 0, half, 3, 0, near(k, True, 3 if u == 1 else 1)).start()
+            if v in (1, 2):
+                half = 2 - v
+                piece_copy(data, ss, rs, k, u, v, half, u, 3, near(k, False, 3 if v == 1 else 1)).start()
+
+    def gather_do(gather, actions):
+        for action in actions:
+            {"start": gather_start, "second": gather_second, "take": gather_take}[action[0]](*gather, *action[1:])
 
     def gather_drain(data, ss, rs):
-        def body(i, _):
-            u, v = i // 4, i % 4
-            for k in range(2):
-                for half in range(2):
-                    piece_copy(data, ss, rs, k, 0, 0, half, u, v, partner).wait_send()
-            return 0
-
         for k in range(2):
-            piece_copy(data, ss, rs, k, 0, 0, l, 0, 0, partner).wait_send()
-        lax.fori_loop(1, 16, body, 0)
+            for u in range(4):
+                for v in range(4):
+                    for half in ((l,) if u == v == 0 else halves(u, v)):
+                        piece_copy(data, ss, rs, k, 0, 0, half, u, v, partner).wait_send()
 
     og = (buf, og_ss, og_rs)
     qd = (qbuf, qd_ss, qd_rs)
@@ -194,10 +212,6 @@
     loads[1].wait()
     gather_start(*og)
 
-    loads[5].wait()
-    loads[6].wait()
-    proj[dp] = lax.dot_general(ad[...], xs[...], NT, preferred_element_type=F32).astype(BF16)
-
     def proj_copy(o, to):
         return pltpu.make_async_remote_copy(
             src_ref=proj.at[dp], dst_ref=proj.at[dp], send_sem=p_ss.at[o], recv_sem=p_rs.at[o],
@@ -207,8 +221,6 @@
     def proj_send(o, _):
         proj_copy(o, None).start()
         return 0
-
-    lax.fori_loop(1, 32, proj_send, 0)
 
     loads[3].wait()
     loads[4].wait()
@@ -287,9 +299,7 @@
 
     lane16 = lax.broadcasted_iota(jnp.int32, (16, 128), 1)
     low = lane16 < 64
-    eye = (
-        lax.broadcasted_iota(jnp.int32, (112, 112), 0) == lax.broadcasted_iota(jnp.int32, (112, 112), 1)
-    ).astype(F32).astype(BF16)
+    low112 = lax.broadcasted_iota(jnp.int32, (112, 128), 1) < 64
 
     def finish(p):
         u, v = piece_uv(p)
@@ -300,23 +310,24 @@
             pair = pair_at(d, u, v)
             e0 = (pair // 4) * 8 + pair % 4
             e1 = e0 + 4
-            rows = jnp.concatenate(
-                [gate[pl.ds(pl.multiple_of(e * 128 + d * 64, 64), 64), :] for e in (e0, e1)], axis=0
-            )
-            gate_t = lax.dot_general(eye, rows, NT, preferred_element_type=F32)
-            up = (hidden * gate_t).astype(BF16)
+            g0, g1 = [gate[:, pl.ds(pl.multiple_of(e * 128, 128), 128)].astype(F32) for e in (e0, e1)]
+            if d == 0:
+                g1 = pltpu.roll(g1, 64, 1)
+            else:
+                g0 = pltpu.roll(g0, 64, 1)
+            up = (hidden * jnp.where(low112, g0, g1)).astype(BF16)
             ft = lax.dot_general(auj[...], up, NN, preferred_element_type=F32)
             turned = pltpu.roll(ft, 64, 1)
             p0, p1 = proj[e0].astype(F32), proj[e1].astype(F32)
             zero = jnp.zeros_like(p0)
             if d == 0:
-                fac[e0, 0:16] += jnp.where(low, ft, 0.0)
-                fac[e1, 0:16] += jnp.where(low, turned, 0.0)
+                fac[e0] += jnp.where(low, ft, 0.0)
+                fac[e1] += jnp.where(low, turned, 0.0)
                 q0 = jnp.where(low, p0, zero)
                 q1 = jnp.where(low, zero, pltpu.roll(p1, 64, 1))
             else:
-                fac[e0, 0:16] += jnp.where(low, 0.0, turned)
-                fac[e1, 0:16] += jnp.where(low, 0.0, ft)
+                fac[e0] += jnp.where(low, 0.0, turned)
+                fac[e1] += jnp.where(low, 0.0, ft)
                 q0 = jnp.where(low, pltpu.roll(p0, 64, 1), zero)
                 q1 = jnp.where(low, zero, p1)
             both = jnp.concatenate([q0, q1], axis=0).astype(BF16)
@@ -326,48 +337,83 @@
             gb[r0, :] += grad[0:16]
             gb[r1, :] += grad[16:32]
 
-    def og_due(s):
-        return jnp.minimum(1 + (4 * s + 2) // 3, 16)
-
-    def qd_due(s):
-        return jnp.clip((s - 11) * 2, 0, 16)
-
-    gather_step(*og, 0)
+    def t1_copy(o):
+        return pltpu.make_async_remote_copy(
+            src_ref=fac.at[(dp + o) % 32], dst_ref=t1.at[o], send_sem=t1_ss.at[o], recv_sem=t1_rs.at[o],
+            device_id={"dp": (dp + o) % 32}, device_id_type=MESH,
+        )
+
+    def t1b_copy(o):
+        return pltpu.make_async_remote_copy(
+            src_ref=sbs.at[(dp + o) % 32], dst_ref=t1b.at[o], send_sem=t1b_ss.at[o], recv_sem=t1b_rs.at[o],
+            device_id={"dp": (dp + o) % 32}, device_id_type=MESH,
+        )
+
+    def hand_over(p):
+        for i, (u, v) in enumerate(ORDER):
+            if ORDER.index((v, u)) > i:
+                continue
+
+            @pl.when(p == i)
+            def _(u=u, v=v):
+                for a, b in {(u, v), (v, u)} if u != v else {(u, u)}:
+                    pair = pair_at(0, a, b)
+                    for half in range(2):
+                        e = (pair // 4 * 2 + half) * 4 + pair % 4
+                        if a == b == 0:
+
+                            @pl.when(half != l)
+                            def _(e=e):
+                                t1_copy((e + 32 - dp) % 32).start()
+                        else:
+                            t1_copy((e + 32 - dp) % 32).start()
+
+    loads[5].wait()
+    loads[6].wait()
+    proj[dp] = lax.dot_general(ad[...], xs[...], NT, preferred_element_type=F32).astype(BF16)
+    gather_take(*og, 0, 0)
 
     def iteration(s, _):
-        @pl.when((s >= 2) & (s - 2 < PIECES))
+        @pl.when((s >= 1 + LAG) & (s - 1 - LAG < PIECES))
         def _():
-            ring_add(s - 2, 1)
-
-        @pl.when((s >= 3) & (s - 3 < PIECES))
+            ring_add(s - 1 - LAG, 1)
+
+        @pl.when((s >= 1 + 2 * LAG) & (s - 1 - 2 * LAG < PIECES))
         def _():
-            ring_add(s - 3, 2)
+            ring_add(s - 1 - 2 * LAG, 2)
 
         @pl.when((s >= 1) & (s - 1 < PIECES))
         def _():
             core_add(s - 1)
 
+        for at, actions in OG_BEFORE.items():
+
+            @pl.when(s == at)
+            def _(actions=actions):
+                gather_do(og, actions)
+
         @pl.when(s < PIECES)
         def _():
             multiply(s)
 
-        def og_step(n, _):
-            gather_step(*og, n)
-            return 0
-
-        lax.fori_loop(og_due(s), og_due(s + 1), og_step, 0)
-
-        @pl.when(s == 11)
+        @pl.when(s < 4)
         def _():
-            loads[9].wait()
-            loads[10].wait()
-            gather_start(*qd)
-
-        def qd_step(n, _):
-            gather_step(*qd, n)
-            return 0
-
-        lax.fori_loop(qd_due(s), qd_due(s + 1), qd_step, 0)
+            lax.fori_loop(jnp.maximum(8 * s, 1), 8 * s + 8, proj_send, 0)
+
+        for at, actions in OG_AFTER.items():
+
+            @pl.when(s == at)
+            def _(actions=actions):
+                gather_do(og, actions)
+
+        for at, actions in QD_AFTER.items():
+
+            @pl.when(s == at)
+            def _(actions=actions):
+                if actions[0][0] == "start":
+                    loads[9].wait()
+                    loads[10].wait()
+                gather_do(qd, actions)
 
         @pl.when(s == STAGES)
         def _():
@@ -380,33 +426,38 @@
         @pl.when(s >= STAGES)
         def _():
             finish(s - STAGES)
+            hand_over(s - STAGES)
 
         return 0
 
     loads[11].wait()
-    qf[...] = qu[...].astype(F32).reshape(2048, 112)
-    for r in range(16):
-        qt[r] = qf[pl.ds(r, 128, stride=16), :].astype(BF16)
-
     lax.fori_loop(0, PIECES + STAGES, iteration, 0)
+
+    def t1_take(o, total):
+        t1_copy(o).wait_recv()
+        return total + t1[o]
+
+    def t2_copy(o):
+        return pltpu.make_async_remote_copy(
+            src_ref=t2s, dst_ref=t2.at[o], send_sem=t2_ss.at[o], recv_sem=t2_rs.at[o],
+            device_id={"tensor": (tn + o) % 8}, device_id_type=MESH,
+        )
+
+    t2s[...] = lax.fori_loop(1, 32, t1_take, fac[dp])
+    for o in range(1, 8):
+        t2_copy(o).start()
 
     score_b = jnp.zeros((32, 128), F32)
     for r in range(16):
         part = gb[pl.ds(r, 32, stride=16), :].astype(BF16)
-        score_b += lax.dot_general(part, qt[r], NT, preferred_element_type=F32)
-    fac[:, 16:24, :] = jnp.broadcast_to(score_b[:, None, :], (32, 8, 128))
-
-    def t1_copy(o):
-        return pltpu.make_async_remote_copy(
-            src_ref=fac.at[(dp + o) % 32], dst_ref=t1.at[o], send_sem=t1_ss.at[o], recv_sem=t1_rs.at[o],
-            device_id={"dp": (dp + o) % 32}, device_id_type=MESH,
-        )
-
-    def t1_send(o, _):
-        t1_copy(o).start()
-        return 0
-
-    lax.fori_loop(1, 32, t1_send, 0)
+        score_b += lax.dot_general(part, qu[r], NN, preferred_element_type=F32)
+    sbs[...] = jnp.broadcast_to(score_b[:, None, :], (32, 8, 128))
+
+    def t1b_send(o, _):
+        t1b_copy(o).start()
+        return 0
+
+    lax.fori_loop(1, 32, t1b_send, 0)
 
     xd = xs[:, pl.ds(pl.multiple_of(tn * width, 128), width)]
 
@@ -421,6 +472,34 @@
         return 0
 
     lax.fori_loop(0, 8, meet, 0)
+    factors = t2s[...]
+    for o in range(1, 8):
+        t2_copy(o).wait_recv()
+        factors += t2[o]
+
+    def t3_copy(o):
+        return pltpu.make_async_remote_copy(
+            src_ref=t3s, dst_ref=t3.at[o], send_sem=t3_ss.at[o], recv_sem=t3_rs.at[o],
+            device_id={"tensor": (tn + o) % 8}, device_id_type=MESH,
+        )
+
+    def weigh(i, _):
+        rows = mt[pl.ds(pl.multiple_of(i * 128, 128), 128), :].reshape(8, 16, 128)
+        acc[pl.ds(pl.multiple_of(i * 8, 8), 8), :] = jnp.sum(rows * factors[None], axis=1)
+        return 0
+
+    lax.fori_loop(0, 16, weigh, 0)
+    score_a = lax.dot_general(
+        jnp.ones((8, 128), F32), acc[...], NT, precision=lax.Precision.HIGHEST, preferred_element_type=F32
+    )
+
+    def t1b_take(o, total):
+        t1b_copy(o).wait_recv()
+        return total + t1b[o]
+
+    t3s[...] = lax.fori_loop(1, 32, t1b_take, sbs[dp] + score_a)
+    for o in range(1, 8):
+        t3_copy(o).start()
     gather_drain(*og)
     gather_drain(*qd)
 
@@ -439,50 +518,12 @@
 
     lax.fori_loop(1, 32, proj_drain, 0)
 
-    def t1_take(o, total):
-        t1_copy(o).wait_recv()
-        return total + t1[o]
-
-    total = lax.fori_loop(1, 32, t1_take, fac[dp])
-
-    def t2_copy(o):
-        return pltpu.make_async_remote_copy(
-            src_ref=t2s, dst_ref=t2.at[o], send_sem=t2_ss.at[o], recv_sem=t2_rs.at[o],
-            device_id={"tensor": (tn + o) % 8}, device_id_type=MESH,
-        )
-
-    def t3_copy(o):
-        return pltpu.make_async_remote_copy(
-            src_ref=t3s, dst_ref=t3.at[o], send_sem=t3_ss.at[o], recv_sem=t3_rs.at[o],
-            device_id={"tensor": (tn + o) % 8}, device_id_type=MESH,
-        )
-
-    t2s[...] = total[0:16]
-    for o in range(1, 8):
-        t2_copy(o).start()
-
     def t1_drain(o, _):
         t1_copy(o).wait_send()
+        t1b_copy(o).wait_send()
         return 0
 
     lax.fori_loop(1, 32, t1_drain, 0)
-    factors = total[0:16]
-    for o in range(1, 8):
-        t2_copy(o).wait_recv()
-        factors += t2[o]
-
-    def weigh(i, _):
-        rows = mt[pl.ds(pl.multiple_of(i * 128, 128), 128), :].reshape(8, 16, 128)
-        acc[pl.ds(pl.multiple_of(i * 8, 8), 8), :] = jnp.sum(rows * factors[None], axis=1)
-        return 0
-
-    lax.fori_loop(0, 16, weigh, 0)
-    score_a = lax.dot_general(
-        jnp.ones((8, 128), F32), acc[...], NT, precision=lax.Precision.HIGHEST, preferred_element_type=F32
-    )
-    t3s[...] = total[16:24] + score_a
-    for o in range(1, 8):
-        t3_copy(o).start()
     for o in range(1, 8):
         t2_copy(o).wait_send()
     scores = t3s[...]
@@ -499,6 +540,8 @@
 
 def shards(x, og, gate, codes, bsc, osc, ad, au, qd, qu):
     qd = qd.reshape(64, 1024)
+    gate = gate.T
+    qu = qu.transpose(1, 2, 0)
     dma = pltpu.SemaphoreType.DMA
     vmem = pltpu.VMEM
     return pl.pallas_call(
@@ -518,10 +561,8 @@
             vmem((16, 8192), BF16),
             vmem((16, 896), BF16),
             vmem((16, 112), BF16),
-            vmem((4096, 112), BF16),
-            vmem((128, 16, 112), BF16),
-            vmem((2048, 112), F32),
-            vmem((16, 128, 112), BF16),
+            vmem((112, 4096), BF16),
+            vmem((16, 112, 128), BF16),
             vmem((8, 112, 256), F32),
             vmem((SLOTS, 4, 112, 256), F32),
             vmem((PIECES, 4, 112, 256), BF16),
@@ -530,10 +571,12 @@
             vmem((PIECES, 2, 3, 112, 128), BF16),
             vmem((32, 16, 128), BF16),
             vmem((512, 112), F32),
-            vmem((32, 24, 128), F32),
-            vmem((32, 24, 128), F32),
+            vmem((32, 16, 128), F32),
+            vmem((32, 16, 128), F32),
             vmem((16, 128), F32),
             vmem((8, 16, 128), F32),
+            vmem((32, 8, 128), F32),
+            vmem((32, 8, 128), F32),
             vmem((2048, 128), F32),
             vmem((128, 128), F32),
             vmem((8, 128), F32),
@@ -551,6 +594,8 @@
             dma((32,)),
             dma((32,)),
             dma((32,)),
+            dma((32,)),
+            dma((32,)),
             dma((8,)),
             dma((8,)),
             dma((8,)),

time: 168 us -> 126 us (0.75)
  Pallas kernels: 163 us -> 125 us
  local copies, waits for them, and re-layouts: 5.64 us -> 1.19 us
    pallas_call x1, Pallas kernels: 163 us -> 125 us  [shards(): pl.pallas_call(kernel, out_shape=jax.ShapeDtypeStruct((1, 16), F32), in_s...]
    unnamed x3 -> x1, local copies, waits for them, and re-layouts: 5.64 us -> 1.19 us
where the time goes in v2:
time: 126 us
  Pallas kernels  125 us (99%)
    pallas_call x1, Pallas kernels, shards(): pl.pallas_call(kernel, out_shape=jax.ShapeDtypeStruct((1, 16), F32), in_s...  125 us

profile of v2, /device:TPU:1, one launch (start us, length us, event | category | flops | bytes accessed | tf_op | source)
XLA Modules:
  0.0 126.4 jit_solution(3958849632778796195)
XLA Ops:
  0.0 125.2 %influence.1 = f32[1,16]{1,0:T(1,128)} custom-call(bf16[128,8192]{1,0:T(8,128)(2,1)} %x_hbm.1, bf16[128,1024]{1,0:T(8,128)(2,1)} %og_hbm.1, bf16[112,4096]{1,0:T(8,128)(2,1)} %bitcast.3, s32[896,1024]{1,0:T(8,128)} %codes_hbm.1, s32[14,1024]{1,0:T(8,128)} %bsc_hbm.1, f32[14,16]{1,0:T(8,128)} %osc_hbm.1, bf16[16,8192]{1,0:T(8,128)(2,1)} %ad_hbm.1, ...), custom_call_target="tpu_custom_call" | custom-call | tf_op jit(solution)/shard_map/influence/pallas_call | solution.py:547
  125.2 1.2 copy.12

commit v3 on v2

v3 whole, which is shorter than its diff:
```python
import jax
import jax.numpy as jnp
from jax import lax
from jax.experimental import pallas as pl
from jax.experimental.pallas import tpu as pltpu
from jax.sharding import PartitionSpec as P

MESH = pl.DeviceIdType.MESH
F32 = jnp.float32
BF16 = jnp.bfloat16
NT = (((1,), (1,)), ((), ()))
NN = (((1,), (0,)), ((), ()))
ANY = pl.BlockSpec(memory_space=pl.ANY)

PIECES = 16
SLOTS = 8
LAG = 2
STAGES = 1 + 3 * LAG

LEVELS = (
    -1.0,
    -0.6961928009986877,
    -0.5250730514526367,
    -0.39491748809814453,
    -0.28444138169288635,
    -0.18477343022823334,
    -0.09105003625154495,
    0.0,
    0.07958029955625534,
    0.16093020141124725,
    0.24611230194568634,
    0.33791524171829224,
    0.44070982933044434,
    0.5626170039176941,
    0.7229568362236023,
    1.0,
)


def lookup(codes):
    values = [jnp.full(codes.shape, level, F32) for level in LEVELS]
    for bit in range(4):
        odd = (codes & (1 << bit)) != 0
        values = [jnp.where(odd, values[i + 1], values[i]) for i in range(0, len(values), 2)]
    return values[0]


def offset(k):
    return k + k // 2 - 2 * (k // 3)


OWN, OTHER = 2, 3
WHOLE = [(0, 0), (3, 0), (0, 3), (1, 1), (1, 2), (2, 1), (2, 2), (1, 3), (3, 1), (3, 2), (2, 3), (3, 3)]
WHOLE = [((u, v, 0), (u, v, 1)) for u, v in WHOLE]
ORDER = [
    ((1, 0, OWN), (2, 0, OWN)),
    WHOLE[0],
    ((0, 1, OWN), (0, 2, OWN)),
    ((1, 0, OTHER), (2, 0, OTHER)),
    ((0, 1, OTHER), (0, 2, OTHER)),
] + WHOLE[1:]
PLACE = {part: i for i, parts in enumerate(ORDER) for part in parts}


def complete_at(p):
    return [(u, v, w) for (u, v, w), i in PLACE.items() if max(i, PLACE[v, u, w]) == p]


def piece_parts(n):
    found = []
    for side in range(2):
        code = pick(n, {i: offset(u) + 4 * offset(v) + 16 * w for i, (u, v, w) in enumerate(parts[side] for parts in ORDER)})
        found.append((code & 3, (code >> 2) & 3, code >> 4))
    return found


def pick(n, table):
    value = 0
    for i, entry in table.items():
        value = jnp.where(n == i, entry, value)
    return value


def takes(*places):
    return [("take", u, v, w) for u, v in places for w in (OWN, OTHER)]


OG_BEFORE = {
    0: [("take", 1, 0, OWN), ("take", 2, 0, OWN)],
    1: [("take", 0, 0, OTHER)],
    3: [("take", 1, 0, OTHER), ("take", 2, 0, OTHER)],
}
OG_AFTER = {
    1: [("take", 0, 1, OWN), ("take", 0, 2, OWN)],
    3: [("take", 0, 1, OTHER), ("take", 0, 2, OTHER), ("second", 1)],
    4: takes((3, 0)) + [("second", 2)],
    5: takes((0, 3)) + [("second", 3)],
    6: [("whole", 1, 1), ("whole", 1, 2)],
    8: [("whole", 2, 1), ("whole", 2, 2)],
    9: takes((1, 3)),
    10: [("whole", 3, 1), ("whole", 3, 2)],
    11: takes((2, 3)),
    13: takes((3, 3)),
}
QD_AFTER = {
    9: [("start",), ("more",)],
    10: [("take", 0, 0, OTHER)],
    12: takes((1, 0), (2, 0), (0, 1), (0, 2)) + [("second", 1), ("second", 2)],
    13: takes((3, 0), (0, 3)) + [("second", 3)],
    14: [("whole", 1, 1), ("whole", 1, 2)],
    15: [("whole", 2, 1), ("whole", 2, 2)],
    17: [("whole", 3, 1), ("whole", 3, 2)] + takes((1, 3)),
    18: takes((2, 3)),
    19: takes((3, 3)),
}
MEET = [(0, 0), (1, 0), (2, 0), (0, 1), (0, 2), (3, 0), (0, 3), (1, 1), (1, 2), (2, 1), (2, 2), (3, 1), (3, 2), (1, 3), (2, 3), (3, 3)]
MET = {10: 1, 12: 5, 13: 7, 14: 9, 15: 11, 17: 14, 18: 15, 19: 16}
EARLY = 12


def kernel(
    x_hbm, og_hbm, gate_hbm, codes_hbm, bsc_hbm, osc_hbm, ad_hbm, au_hbm, qd_hbm, qu_hbm,
    out_ref,
    buf, qbuf, codes, bsc, osc, scale, w, xs, ad, au, auj, gate, qu,
    prod, csend, crecv, rsend, rrecv, proj, gb, fac, t1, t2s, t2, sbs, sbl, t1b, mt, acc, t3s, t3,
    lsem, og_ss, og_rs, qd_ss, qd_rs, c_ss, c_rs, r_ss, r_rs, p_ss, p_rs, t1_ss, t1_rs, t1b_ss, t1b_rs, t2_ss, t2_rs, t3_ss, t3_rs,
):
    dp = lax.axis_index("dp")
    tn = lax.axis_index("tensor")
    y, l, x = dp & 3, (dp >> 2) & 1, dp >> 3
    zh, c = tn >> 1, tn & 1

    width = og_hbm.shape[1]
    here = x * 4 + y
    loads = [
        (og_hbm.at[pl.ds(0, 64)], buf.at[0, here, l]),
        (og_hbm.at[pl.ds(64, 64)], buf.at[1, here, l]),
        (codes_hbm, codes),
        (bsc_hbm, bsc),
        (osc_hbm, osc),
        (x_hbm, xs),
        (ad_hbm, ad),
        (au_hbm, au),
        (gate_hbm, gate),
        (qd_hbm.at[pl.ds(0, 32)], qbuf.at[0, here, l]),
        (qd_hbm.at[pl.ds(32, 32)], qbuf.at[1, here, l]),
        (qu_hbm, qu),
    ]
    loads = [pltpu.make_async_copy(a, b, lsem.at[i]) for i, (a, b) in enumerate(loads)]
    for load in loads:
        load.start()

    barrier = pltpu.get_barrier_semaphore()

    def greet_dp(o, _):
        pl.semaphore_signal(barrier, 1, device_id={"dp": ((dp + o) & 31)}, device_id_type=MESH)
        return 0

    def greet_tn(o, _):
        pl.semaphore_signal(barrier, 1, device_id={"tensor": ((tn + o) & 7)}, device_id_type=MESH)
        return 0

    lax.fori_loop(1, 32, greet_dp, 0)
    lax.fori_loop(1, 8, greet_tn, 0)
    pl.semaphore_wait(barrier, 38)

    def pair_of(k, a, b):
        if k == 1:
            a, b = b, a
        return ((x + a) & 3) * 4 + ((y + b) & 3)

    def pair_at(k, u, v):
        return pair_of(k, offset(u), offset(v))

    def near(k, first, step):
        along_x = first == (k == 0)
        if along_x:
            return {"dp": (((x + step) & 3) * 2 + l) * 4 + y}
        return {"dp": (x * 2 + l) * 4 + ((y + step) & 3)}

    def piece_copy(data, ss, rs, k, u, v, half, ur, vr, target):
        ref = data.at[k, pair_at(k, u, v)]
        sem = 0 if half is None else half
        ref = ref if half is None else ref.at[half]
        return pltpu.make_async_remote_copy(
            src_ref=ref, dst_ref=ref, send_sem=ss.at[k, ur, vr, sem], recv_sem=rs.at[k, ur, vr, sem],
            device_id=target, device_id_type=MESH,
        )

    partner = {"dp": (x * 2 + 1 - l) * 4 + y}

    def half_of(w):
        if isinstance(w, int):
            return w if w < 2 else l if w == OWN else 1 - l
        return jnp.where(w < 2, w, jnp.where(w == OWN, l, 1 - l))

    def gather_first(data, ss, rs, k, half):
        piece_copy(data, ss, rs, k, 0, 0, half, 2, 0, near(k, True, 1)).start()
        piece_copy(data, ss, rs, k, 0, 0, half, 1, 0, near(k, True, 3)).start()

    def gather_more(data, ss, rs, half=None):
        half = l if half is None else half
        for k in range(2):
            piece_copy(data, ss, rs, k, 0, 0, half, 0, 2, near(k, False, 1)).start()
            piece_copy(data, ss, rs, k, 0, 0, half, 0, 1, near(k, False, 3)).start()

    def gather_start(data, ss, rs):
        for k in range(2):
            piece_copy(data, ss, rs, k, 0, 0, l, 0, 0, partner).start()
            gather_first(data, ss, rs, k, l)

    def gather_second(data, ss, rs, u):
        for k in range(2):
            piece_copy(data, ss, rs, k, u, 0, None, u, 2, near(k, False, 1)).start()
            piece_copy(data, ss, rs, k, u, 0, None, u, 1, near(k, False, 3)).start()

    def gather_take(data, ss, rs, u, v, w):
        half = half_of(w)
        for k in range(2):
            piece_copy(data, ss, rs, k, u, v, half, u, v, partner).wait_recv()
            if (u, v) == (0, 0):
                gather_first(data, ss, rs, k, half)
            if (u, v) in ((1, 0), (2, 0), (0, 1), (0, 2)):
                step, at = (3, 1) if 1 in (u, v) else (1, 0)
                ur, vr = (3, 0) if v == 0 else (0, 3)

                @pl.when(half == at)
                def _(k=k, step=step, at=at, ur=ur, vr=vr):
                    piece_copy(data, ss, rs, k, u, v, at, ur, vr, near(k, v == 0, step)).start()
        if (u, v) == (0, 0):
            gather_more(data, ss, rs, half)

    def gather_whole(data, ss, rs, u, v):
        for k in range(2):
            piece_copy(data, ss, rs, k, u, v, None, u, v, partner).wait_recv()
            step, at = (3, 1) if v == 1 else (1, 0)
            piece_copy(data, ss, rs, k, u, v, at, u, 3, near(k, False, step)).start()

    def gather_do(gather, actions):
        for action in actions:
            act = {
                "start": gather_start, "more": gather_more, "second": gather_second,
                "take": gather_take, "whole": gather_whole,
            }[action[0]]
            act(*gather, *action[1:])

    def gather_drain(data, ss, rs):
        for k in range(2):
            for u in range(4):
                for v in range(4):
                    pieces = (l,) if u == v == 0 else (0, 1) if u == 0 or v in (0, 3) else (None,)
                    for half in pieces:
                        piece_copy(data, ss, rs, k, 0, 0, half, u, v, partner).wait_send()

    og = (buf, og_ss, og_rs)
    qd = (qbuf, qd_ss, qd_rs)
    loads[0].wait()
    loads[1].wait()
    gather_start(*og)

    loads[3].wait()
    loads[4].wait()
    lane14 = lax.broadcasted_iota(jnp.int32, (14, 128), 1)
    for col in range(width // 128):
        column = jnp.where(
            lane14 < 64,
            jnp.broadcast_to(osc[:, 2 * col : 2 * col + 1], (14, 128)),
            jnp.broadcast_to(osc[:, 2 * col + 1 : 2 * col + 2], (14, 128)),
        )
        at = pl.ds(col * 128, 128)
        scale[:, at] = (bsc[:, at] + 1).astype(F32) / 256.0 * column
    loads[2].wait()

    def dequant(b, _):
        rows = pl.ds(pl.multiple_of(b * 64, 64), 64)
        w[rows, :] = (lookup(codes[rows, :]) * scale[pl.ds(b, 1), :]).astype(BF16)
        return 0

    lax.fori_loop(0, 8, dequant, 0)
    gather_more(*og)
    lax.fori_loop(8, 14, dequant, 0)


    loads[7].wait()
    mine = jnp.zeros((16, 112), F32)
    for j in range(8):
        mine = jnp.where(tn == j, au[:, j * 112 : (j + 1) * 112].astype(F32), mine)
    auj[...] = mine.astype(BF16)
    gb[...] = jnp.zeros_like(gb)
    fac[...] = jnp.zeros_like(fac)
    loads[8].wait()


    def project():
        proj[dp] = lax.dot_general(ad[...], xs[...], NT, preferred_element_type=F32).astype(BF16)

    for i in (5, 6, 9, 10, 11):
        loads[i].wait()

    def proj_copy(o, to):
        return pltpu.make_async_remote_copy(
            src_ref=proj.at[dp], dst_ref=proj.at[dp], send_sem=p_ss.at[o], recv_sem=p_rs.at[o],
            device_id={"dp": ((dp + o) & 31)}, device_id_type=MESH,
        )

    def proj_send(o, _):
        proj_copy(o, None).start()
        return 0

    def core_copy(p):
        return pltpu.make_async_remote_copy(
            src_ref=csend.at[p], dst_ref=crecv.at[p], send_sem=c_ss.at[p], recv_sem=c_rs.at[p],
            device_id={"tensor": zh * 2 + 1 - c}, device_id_type=MESH,
        )

    def ring_copy(p, d, i):
        step = 1 if d == 0 else 3
        return pltpu.make_async_remote_copy(
            src_ref=rsend.at[p, d, i], dst_ref=rrecv.at[p, d, i], send_sem=r_ss.at[p, d, i],
            recv_sem=r_rs.at[p, d, i],
            device_id={"tensor": ((zh + step) & 3) * 2 + c}, device_id_type=MESH,
        )

    def ring_target(d, i):
        return (zh + (3 - i if d == 0 else i + 1)) & 3

    def multiply(p):
        parts = piece_parts(p)
        rows = jnp.concatenate(
            [buf[k, pair_of(k, a, b), half_of(w)] for k in range(2) for a, b, w in parts], axis=0
        )
        slot = (p & (SLOTS - 1))
        prod[slot] = lax.dot_general(w[...], rows, NT, preferred_element_type=F32).reshape(8, 112, 256)
        for k in range(4):
            csend[p, k] = prod[slot, 2 * k + 1 - c].astype(BF16)
        core_copy(p).start()

    def chip_sum(p, d, k):
        at = slice(d * 128, (d + 1) * 128)
        return prod[(p & (SLOTS - 1)), 2 * k + c, :, at] + crecv[p, k, :, at].astype(F32)

    def core_add(p):
        core_copy(p).wait_recv()
        for d in range(2):
            rsend[p, d, 0] = chip_sum(p, d, ring_target(d, 0)).astype(BF16)
            ring_copy(p, d, 0).start()

    def ring_add(p, i):
        for d in range(2):
            ring_copy(p, d, i - 1).wait_recv()
            part = chip_sum(p, d, ring_target(d, i))
            rsend[p, d, i] = (part + rrecv[p, d, i - 1].astype(F32)).astype(BF16)
            ring_copy(p, d, i).start()

    lane16 = lax.broadcasted_iota(jnp.int32, (16, 128), 1)
    low = lane16 < 64
    low112 = lax.broadcasted_iota(jnp.int32, (112, 128), 1) < 64

    def example_at(pair, half):
        return (pair >> 2) * 8 + half * 4 + (pair & 3)

    def finish(p):
        parts = piece_parts(p)
        for d in range(2):
            ring_copy(p, d, 2).wait_recv()
        sums = []
        for d in range(2):
            hidden = chip_sum(p, d, zh) + rrecv[p, d, 2].astype(F32)
            e0, e1 = [example_at(pair_of(d, a, b), half_of(w)) for a, b, w in parts]
            g0, g1 = [gate[:, pl.ds(pl.multiple_of(e * 128, 128), 128)].astype(F32) for e in (e0, e1)]
            p0, p1 = proj[e0].astype(F32), proj[e1].astype(F32)
            if d == 0:
                g1 = pltpu.roll(g1, 64, 1)
                p1 = pltpu.roll(p1, 64, 1)
            else:
                g0 = pltpu.roll(g0, 64, 1)
                p0 = pltpu.roll(p0, 64, 1)
            up = (hidden * jnp.where(low112, g0, g1)).astype(BF16)
            both = jnp.concatenate([jnp.where(low, p0, 0.0), jnp.where(low, 0.0, p1)], axis=0).astype(BF16)
            ft = lax.dot_general(auj[...], up, NN, preferred_element_type=F32)
            grad = lax.dot_general(both, up, NT, preferred_element_type=F32)
            sums.append((e0, e1, ft, grad))
        for d, (e0, e1, ft, grad) in enumerate(sums):
            turned = pltpu.roll(ft, 64, 1)
            if d == 0:
                fac[e0] += jnp.where(low, ft, 0.0)
                fac[e1] += jnp.where(low, turned, 0.0)
            else:
                fac[e0] += jnp.where(low, 0.0, turned)
                fac[e1] += jnp.where(low, 0.0, ft)
            gb[pl.ds(pl.multiple_of(e0 * 16, 16), 16), :] += grad[0:16]
            gb[pl.ds(pl.multiple_of(e1 * 16, 16), 16), :] += grad[16:32]

    def t1_copy(o):
        return pltpu.make_async_remote_copy(
            src_ref=fac.at[((dp + o) & 31)], dst_ref=t1.at[o], send_sem=t1_ss.at[o], recv_sem=t1_rs.at[o],
            device_id={"dp": ((dp + o) & 31)}, device_id_type=MESH,
        )

    def t1b_copy(o, rows=sbs):
        return pltpu.make_async_remote_copy(
            src_ref=rows.at[((dp + o) & 31)], dst_ref=t1b.at[o], send_sem=t1b_ss.at[o], recv_sem=t1b_rs.at[o],
            device_id={"dp": ((dp + o) & 31)}, device_id_type=MESH,
        )

    def send_each(copy, places):
        for u, v, w in places:
            e = example_at(pair_at(0, u, v), half_of(w))
            if u == v == 0:

                @pl.when(half_of(w) != l)
                def _(e=e):
                    copy((e + 32 - dp) & 31).start()
            else:
                copy((e + 32 - dp) & 31).start()

    def hand_over(p):
        for i in range(PIECES):
            if complete_at(i):

                @pl.when(p == i)
                def _(i=i):
                    send_each(t1_copy, complete_at(i))

    def score_up():
        score_b = jnp.zeros((32, 128), F32)
        for r in range(16):
            part = gb[pl.ds(r, 32, stride=16), :].astype(BF16)
            score_b += lax.dot_general(part, qu[r], NN, preferred_element_type=F32)
        return jnp.broadcast_to(score_b[:, None, :], (32, 8, 128))

    def meet(n, _):
        xd = xs[:, pl.ds(pl.multiple_of(tn * width, 128), width)]
        a, b = [pick(n, {i: offset(place[j]) for i, place in enumerate(MEET)}) for j in range(2)]
        pairs = [pair_of(k, a, b) for k in range(2)]
        rows = jnp.concatenate([qbuf[k, pairs[k]].reshape(64, width) for k in range(2)], axis=0)
        part = lax.dot_general(rows, xd, NT, preferred_element_type=F32).reshape(2, 2, 32, 128)
        for k in range(2):
            for half in range(2):
                start = example_at(pairs[k], half) * 64 + k * 32
                mt[pl.ds(pl.multiple_of(start, 32), 32), :] = part[k, half]
        return 0

    def proj_drain(o, _):
        proj_copy(o, None).wait_send()
        return 0

    def met(s):
        count = 0
        for at, n in MET.items():
            count = jnp.where(s > at, n, count)
        return count

    def iteration(s, _):
        @pl.when((s >= 1 + LAG) & (s - 1 - LAG < PIECES))
        def _():
            ring_add(s - 1 - LAG, 1)

        @pl.when((s >= 1 + 2 * LAG) & (s - 1 - 2 * LAG < PIECES))
        def _():
            ring_add(s - 1 - 2 * LAG, 2)

        @pl.when((s >= 1) & (s - 1 < PIECES))
        def _():
            core_add(s - 1)

        @pl.when(s < 4)
        def _():
            for at, actions in OG_BEFORE.items():

                @pl.when(s == at)
                def _(actions=actions):
                    gather_do(og, actions)

        @pl.when(s < PIECES)
        def _():
            multiply(s)

        @pl.when(s == 1)
        def _():
            project()

        @pl.when((s >= 2) & (s < 6))
        def _():
            lax.fori_loop(jnp.maximum(8 * s - 16, 1), 8 * s - 8, proj_send, 0)

        for low_s in range(0, PIECES + STAGES, 6):

            @pl.when((s >= low_s) & (s < low_s + 6))
            def _(low_s=low_s):
                for at in range(low_s, low_s + 6):
                    if at in OG_AFTER or at in QD_AFTER:

                        @pl.when(s == at)
                        def _(at=at):
                            gather_do(og, OG_AFTER.get(at, ()))
                            gather_do(qd, QD_AFTER.get(at, ()))

        @pl.when(s == STAGES)
        def _():
            def proj_wait(o, _):
                proj_copy(o, None).wait_recv()
                return 0

            lax.fori_loop(1, 32, proj_wait, 0)

        @pl.when(s >= STAGES)
        def _():
            finish(s - STAGES)
            hand_over(s - STAGES)
            core_copy(s - STAGES).wait_send()
            for d in range(2):
                for i in range(3):
                    ring_copy(s - STAGES, d, i).wait_send()

        @pl.when(s == 10)
        def _():
            lax.fori_loop(1, 32, proj_drain, 0)

        @pl.when(s == 17)
        def _():
            gather_drain(*og)

        lax.fori_loop(met(s), met(s + 1), meet, 0)

        @pl.when(s == STAGES + EARLY)
        def _():
            sbs[...] = score_up()
            send_each(t1b_copy, [e for i in range(EARLY + 1) for e in complete_at(i)])

        return 0

    lax.fori_loop(0, PIECES + STAGES, iteration, 0)

    def t1_take(o, total):
        t1_copy(o).wait_recv()
        return total + t1[o]

    def t2_copy(o):
        return pltpu.make_async_remote_copy(
            src_ref=t2s, dst_ref=t2.at[o], send_sem=t2_ss.at[o], recv_sem=t2_rs.at[o],
            device_id={"tensor": ((tn + o) & 7)}, device_id_type=MESH,
        )

    t2s[...] = lax.fori_loop(1, 32, t1_take, fac[dp])
    for o in range(1, 8):
        t2_copy(o).start()

    late = [e for i in range(EARLY + 1, PIECES) for e in complete_at(i)]
    sbl[...] = score_up()
    send_each(lambda o: t1b_copy(o, sbl), late)

    factors = t2s[...]
    for o in range(1, 8):
        t2_copy(o).wait_recv()
        factors += t2[o]

    def t3_copy(o):
        return pltpu.make_async_remote_copy(
            src_ref=t3s, dst_ref=t3.at[o], send_sem=t3_ss.at[o], recv_sem=t3_rs.at[o],
            device_id={"tensor": ((tn + o) & 7)}, device_id_type=MESH,
        )

    def weigh(i, _):
        rows = mt[pl.ds(pl.multiple_of(i * 128, 128), 128), :].reshape(8, 16, 128)
        acc[pl.ds(pl.multiple_of(i * 8, 8), 8), :] = jnp.sum(rows * factors[None], axis=1)
        return 0

    lax.fori_loop(0, 16, weigh, 0)
    score_a = lax.dot_general(
        jnp.ones((8, 128), F32), acc[...], NT, precision=lax.Precision.HIGHEST, preferred_element_type=F32
    )

    def t1b_take(o, total):
        t1b_copy(o).wait_recv()
        return total + t1b[o]

    t3s[...] = lax.fori_loop(1, 32, t1b_take, sbs[dp] + score_a)
    for o in range(1, 8):
        t3_copy(o).start()
    gather_drain(*qd)

    def t1_drain(o, _):
        t1_copy(o).wait_send()
        t1b_copy(o).wait_send()
        return 0

    lax.fori_loop(1, 32, t1_drain, 0)
    for o in range(1, 8):
        t2_copy(o).wait_send()
    scores = t3s[...]
    for o in range(1, 8):
        t3_copy(o).wait_recv()
        scores += t3[o]
    out = jnp.zeros((1, 16), F32)
    for j in range(8):
        out = jnp.where(tn == j, scores[0:1, j * 16 : (j + 1) * 16], out)
    out_ref[...] = out
    for o in range(1, 8):
        t3_copy(o).wait_send()


def shards(x, og, gate, codes, bsc, osc, ad, au, qd, qu):
    qd = qd.reshape(64, 1024)
    gate = gate.T
    qu = qu.transpose(1, 2, 0)
    dma = pltpu.SemaphoreType.DMA
    vmem = pltpu.VMEM
    return pl.pallas_call(
        kernel,
        out_shape=jax.ShapeDtypeStruct((1, 16), F32),
        in_specs=[ANY] * 10,
        out_specs=pl.BlockSpec(memory_space=pltpu.VMEM),
        scratch_shapes=[
            vmem((2, 16, 2, 64, 1024), BF16),
            vmem((2, 16, 2, 32, 1024), BF16),
            vmem((896, 1024), jnp.int32),
            vmem((14, 1024), jnp.int32),
            vmem((14, 16), F32),
            vmem((14, 1024), F32),
            vmem((896, 1024), BF16),
            vmem((128, 8192), BF16),
            vmem((16, 8192), BF16),
            vmem((16, 896), BF16),
            vmem((16, 112), BF16),
            vmem((112, 4096), BF16),
            vmem((16, 112, 128), BF16),
            vmem((SLOTS, 8, 112, 256), F32),
            vmem((PIECES, 4, 112, 256), BF16),
            vmem((PIECES, 4, 112, 256), BF16),
            vmem((PIECES, 2, 3, 112, 128), BF16),
            vmem((PIECES, 2, 3, 112, 128), BF16),
            vmem((32, 16, 128), BF16),
            vmem((512, 112), F32),
            vmem((32, 16, 128), F32),
            vmem((32, 16, 128), F32),
            vmem((16, 128), F32),
            vmem((8, 16, 128), F32),
            vmem((32, 8, 128), F32),
            vmem((32, 8, 128), F32),
            vmem((32, 8, 128), F32),
            vmem((2048, 128), F32),
            vmem((128, 128), F32),
            vmem((8, 128), F32),
            vmem((8, 8, 128), F32),
            dma((12,)),
            dma((2, 4, 4, 2)),
            dma((2, 4, 4, 2)),
            dma((2, 4, 4, 2)),
            dma((2, 4, 4, 2)),
            dma((PIECES,)),
            dma((PIECES,)),
            dma((PIECES, 2, 3)),
            dma((PIECES, 2, 3)),
            dma((32,)),
            dma((32,)),
            dma((32,)),
            dma((32,)),
            dma((32,)),
            dma((32,)),
            dma((8,)),
            dma((8,)),
            dma((8,)),
            dma((8,)),
        ],
        compiler_params=pltpu.CompilerParams(
            collective_id=0, has_side_effects=True, vmem_limit_bytes=60 * 1024 * 1024
        ),
        name="influence",
    )(x, og, gate, codes, bsc, osc, ad, au, qd, qu)


def solution(mesh):
    in_specs = (
        P("dp", None),
        P("dp", "tensor"),
        P(None, ("dp", "tensor")),
        P("dp", "tensor"),
        P("dp", "tensor"),
        P("dp", "tensor"),
        P(),
        P(None, "dp"),
        P("dp", None, "tensor"),
        P(None, None, ("dp", "tensor")),
    )
    return jax.shard_map(shards, mesh=mesh, in_specs=in_specs, out_specs=P("dp", "tensor"), check_vma=False)
```

time: 126 us -> 124 us (0.984)
  Pallas kernels: 125 us -> 122 us
    pallas_call x1, Pallas kernels: 125 us -> 122 us  [shards(): pl.pallas_call(kernel, out_shape=jax.ShapeDtypeStruct((1, 16), F32), in_s...]
where the time goes in v3:
time: 124 us; the launch traced here: 123 us
  Pallas kernels  122 us (98%)
    pallas_call x1, Pallas kernels, shards(): pl.pallas_call(kernel, out_shape=jax.ShapeDtypeStruct((1, 16), F32), in_s...  122 us

profile of v3, /device:TPU:1, one launch (start us, length us, event | category | flops | bytes accessed | tf_op | source)
XLA Modules:
  0.0 123.5 jit_solution(11788139710747124072)
XLA Ops:
  0.0 122.3 %influence.1 = f32[1,16]{1,0:T(1,128)} custom-call(bf16[128,8192]{1,0:T(8,128)(2,1)} %x_hbm.1, bf16[128,1024]{1,0:T(8,128)(2,1)} %og_hbm.1, bf16[112,4096]{1,0:T(8,128)(2,1)} %bitcast.3, s32[896,1024]{1,0:T(8,128)} %codes_hbm.1, s32[14,1024]{1,0:T(8,128)} %bsc_hbm.1, f32[14,16]{1,0:T(8,128)} %osc_hbm.1, bf16[16,8192]{1,0:T(8,128)(2,1)} %ad_hbm.1, ...), custom_call_target="tpu_custom_call" | custom-call | tf_op jit(solution)/shard_map/influence/pallas_call | solution.py:609
  122.3 1.2 copy.12

commit v4 on v3

--- a/solution.py
+++ b/solution.py
@@ -93,28 +93,28 @@
 OG_AFTER = {
     1: [("take", 0, 1, OWN), ("take", 0, 2, OWN)],
     3: [("take", 0, 1, OTHER), ("take", 0, 2, OTHER), ("second", 1)],
-    4: takes((3, 0)) + [("second", 2)],
-    5: takes((0, 3)) + [("second", 3)],
-    6: [("whole", 1, 1), ("whole", 1, 2)],
+    4: takes((3, 0)),
+    5: takes((0, 3)) + [("second", 2)],
+    6: [("whole", 1, 1), ("whole", 1, 2), ("second", 3)],
     8: [("whole", 2, 1), ("whole", 2, 2)],
-    9: takes((1, 3)),
-    10: [("whole", 3, 1), ("whole", 3, 2)],
-    11: takes((2, 3)),
-    13: takes((3, 3)),
+    10: takes((1, 3)),
+    11: [("whole", 3, 1), ("whole", 3, 2)],
+    12: takes((2, 3)),
+    14: takes((3, 3)),
 }
 QD_AFTER = {
-    9: [("start",), ("more",)],
-    10: [("take", 0, 0, OTHER)],
-    12: takes((1, 0), (2, 0), (0, 1), (0, 2)) + [("second", 1), ("second", 2)],
-    13: takes((3, 0), (0, 3)) + [("second", 3)],
-    14: [("whole", 1, 1), ("whole", 1, 2)],
-    15: [("whole", 2, 1), ("whole", 2, 2)],
-    17: [("whole", 3, 1), ("whole", 3, 2)] + takes((1, 3)),
-    18: takes((2, 3)),
-    19: takes((3, 3)),
+    10: [("start",), ("more",)],
+    11: [("take", 0, 0, OTHER)],
+    13: takes((1, 0), (2, 0), (0, 1), (0, 2)) + [("second", 1), ("second", 2)],
+    14: takes((3, 0), (0, 3)) + [("second", 3)],
+    15: [("whole", 1, 1), ("whole", 1, 2)],
+    16: [("whole", 2, 1), ("whole", 2, 2)],
+    18: [("whole", 3, 1), ("whole", 3, 2)] + takes((1, 3)),
+    19: takes((2, 3)),
+    20: takes((3, 3)),
 }
 MEET = [(0, 0), (1, 0), (2, 0), (0, 1), (0, 2), (3, 0), (0, 3), (1, 1), (1, 2), (2, 1), (2, 2), (3, 1), (3, 2), (1, 3), (2, 3), (3, 3)]
-MET = {10: 1, 12: 5, 13: 7, 14: 9, 15: 11, 17: 14, 18: 15, 19: 16}
+MET = {11: 1, 13: 5, 14: 7, 15: 9, 16: 11, 18: 14, 19: 15, 20: 16}
 EARLY = 12
 
 

time: 124 us -> 119 us (0.960)
  Pallas kernels: 122 us -> 118 us
    pallas_call x1, Pallas kernels: 122 us -> 118 us  [shards(): pl.pallas_call(kernel, out_shape=jax.ShapeDtypeStruct((1, 16), F32), in_s...]
where the time goes in v4:
time: 119 us
  Pallas kernels  118 us (99%)
  local copies, waits for them, and re-layouts  1.19 us (1%)
    pallas_call x1, Pallas kernels, shards(): pl.pallas_call(kernel, out_shape=jax.ShapeDtypeStruct((1, 16), F32), in_s...  118 us

profile of v4, /device:TPU:1, one launch (start us, length us, event | category | flops | bytes accessed | tf_op | source)
XLA Modules:
  0.0 119.0 jit_solution(5223783167530682630)
XLA Ops:
  0.0 117.8 %influence.1 = f32[1,16]{1,0:T(1,128)} custom-call(bf16[128,8192]{1,0:T(8,128)(2,1)} %x_hbm.1, bf16[128,1024]{1,0:T(8,128)(2,1)} %og_hbm.1, bf16[112,4096]{1,0:T(8,128)(2,1)} %bitcast.3, s32[896,1024]{1,0:T(8,128)} %codes_hbm.1, s32[14,1024]{1,0:T(8,128)} %bsc_hbm.1, f32[14,16]{1,0:T(8,128)} %osc_hbm.1, bf16[16,8192]{1,0:T(8,128)(2,1)} %ad_hbm.1, ...), custom_call_target="tpu_custom_call" | custom-call | tf_op jit(solution)/shard_map/influence/pallas_call | solution.py:609
  117.8 1.2 %copy.12 = f32[1,16]{1,0:T(1,128)} copy(f32[1,16]{1,0:T(1,128)} %influence.1) | data formatting | bytes 128
